TPU v7x, 256 devices: a whole 4x4x8 slice. The times are simulated.
256 devices in a mesh: section: 2 (over y_lo), tp: 4 (over x), ep: 32 (over z, y_hi, core).
Axes of the slice: x: 4, y: 4 (y_hi: 2, y_lo: 2; y = y_hi * 2 + y_lo), z: 8, core: 2. Of those that a mesh axis runs over, the one named last changes fastest.
Arguments:
- tokens: bfloat16 [4096, 5120], P(('tp', 'ep'), 'section'), may hold values from -160 to 160
- gain: float32 [5120], P('section'), may hold values from 0.4 to 2.5
- routes: int32 [4096, 6], P(('tp', 'ep')), may hold values from 0 to 127, all different within a row; in each aligned block of 32 rows (0 to 31, 32 to 63, ...) at most 2 rows name the same one
- route_weights: float32 [4096, 6], P(('tp', 'ep')), may hold values from 0.03 to 0.5
- w_gate: bfloat16 [128, 5120, 768], P(('tp', 'ep'), 'section'), may hold values from -0.078125 to 0.078125
- w_up: bfloat16 [128, 5120, 768], P(('tp', 'ep'), 'section'), may hold values from -0.078125 to 0.078125
- w_down: bfloat16 [128, 768, 5120], P(('tp', 'ep'), None, 'section'), may hold values from -0.21875 to 0.21875
- grad_out: bfloat16 [4096, 5120], P(('tp', 'ep'), 'section'), may hold values from -6 to 6
Outputs:
- routed: bfloat16 [4096, 5120], P(('tp', 'ep'), 'section')
- grad_tokens: bfloat16 [4096, 5120], P(('tp', 'ep'), 'section')
- grad_weights: float32 [4096, 6], P(('tp', 'ep'))
Inputs may be any that keep to these rules, and one draw needn't show every extreme that they name: `routes`: each row names 6 different experts. In each aligned block of 32 rows (the rows of one index of tp and ep) no expert is named by more than 2 rows, a bound that some block reaches.
All inputs are finite; a program needn't handle non-finite values.
Results may differ from a plain program's by a relative error of at most 0.0072.
Values may be sent and summed in bfloat16 or wider, within the bound.
No kernel may reach another device: no remote copies, remote signals or barrier semaphores. Data moves between devices by JAX's collectives and lax.ppermute only.
A program may use at most 64 MiB of HBM per device.

v0:
```python
import jax
import jax.numpy as jnp
from jax import lax
from jax.sharding import PartitionSpec as P

EPS = 1e-06


def contract_last(left, right):
    return lax.dot_general(
        left, right, (((1,), (1,)), ((), ())), preferred_element_type=jnp.float32
    )


def contract_first(left, right):
    return lax.dot_general(
        left, right, (((0,), (0,)), ((), ())), preferred_element_type=jnp.float32
    )


def to_experts(outgoing, tp_size, ep_size, cap_src):
    model_dim = outgoing.shape[1]
    blocked = outgoing.reshape(tp_size * ep_size, cap_src, model_dim)
    received = lax.all_to_all(blocked, ("tp", "ep"), split_axis=0, concat_axis=0, tiled=True)
    return received.reshape(-1, model_dim)


def from_experts(results, tp_size, ep_size, cap_src):
    model_dim = results.shape[1]
    blocked = results.reshape(tp_size * ep_size, cap_src, model_dim)
    received = lax.all_to_all(blocked, ("tp", "ep"), split_axis=0, concat_axis=0, tiled=True)
    return received.reshape(-1, model_dim)


def local(tokens, gain, routes, route_weights, w_gate, w_up, w_down, grad_out):
    tok_dev, half_dim = tokens.shape
    top_k = routes.shape[1]
    tp_size = lax.axis_size("tp")
    ep_size = lax.axis_size("ep")
    section_size = lax.axis_size("section")
    full_dim = half_dim * section_size
    experts = tp_size * ep_size
    cap_src = max(2, tok_dev * top_k // experts + 1)
    assigns = tok_dev * top_k
    gate_mat, up_mat, down_mat = (w_gate[0], w_up[0], w_down[0])
    ff_dim = gate_mat.shape[1]
    tokens_f = tokens.astype(jnp.float32)
    squares = lax.psum(jnp.sum(tokens_f * tokens_f, axis=1, keepdims=True), "section")
    inv_rms = lax.rsqrt(squares / full_dim + EPS)
    normed = (tokens_f * inv_rms * gain).astype(jnp.bfloat16)
    flat_routes = routes.reshape(-1)
    onehot = (flat_routes[:, None] == jnp.arange(experts, dtype=jnp.int32)[None, :]).astype(
        jnp.int32
    )
    before = jnp.cumsum(onehot, axis=0) - onehot
    slot_rank = jnp.sum(before * onehot, axis=1)
    target = flat_routes * cap_src + slot_rank
    placement = (jnp.arange(experts * cap_src, dtype=jnp.int32)[:, None] == target[None, :]).astype(
        jnp.bfloat16
    )
    outgoing = jnp.dot(
        placement, jnp.repeat(normed, top_k, axis=0), preferred_element_type=jnp.float32
    ).astype(jnp.bfloat16)
    arrived = to_experts(outgoing, tp_size, ep_size, cap_src)
    partial_pre = jnp.concatenate(
        [
            jnp.dot(arrived, gate_mat, preferred_element_type=jnp.float32),
            jnp.dot(arrived, up_mat, preferred_element_type=jnp.float32),
        ],
        axis=1,
    )
    joined = lax.psum(partial_pre, "section")
    pre_gate = joined[:, :ff_dim]
    pre_up = joined[:, ff_dim:]
    sigmoid_gate = jax.nn.sigmoid(pre_gate)
    activated = (pre_gate * sigmoid_gate * pre_up).astype(jnp.bfloat16)
    expert_out = jnp.dot(activated, down_mat, preferred_element_type=jnp.float32).astype(
        jnp.bfloat16
    )
    returned = from_experts(expert_out, tp_size, ep_size, cap_src)
    per_token = contract_first(placement, returned).reshape(tok_dev, top_k, half_dim)
    routed = jnp.sum(route_weights[:, :, None] * per_token, axis=1).astype(jnp.bfloat16)
    grad_f = grad_out.astype(jnp.float32)
    weight_partial = jnp.sum(grad_f[:, None, :] * per_token, axis=2)
    grad_expert = (
        (route_weights[:, :, None] * grad_f[:, None, :])
        .astype(jnp.bfloat16)
        .reshape(assigns, half_dim)
    )
    grad_outgoing = jnp.dot(placement, grad_expert, preferred_element_type=jnp.float32).astype(
        jnp.bfloat16
    )
    grad_arrived = to_experts(grad_outgoing, tp_size, ep_size, cap_src)
    grad_act = lax.psum(contract_last(grad_arrived, down_mat), "section")
    grad_gate = (grad_act * pre_up * sigmoid_gate * (1.0 + pre_gate * (1.0 - sigmoid_gate))).astype(
        jnp.bfloat16
    )
    grad_up = (grad_act * pre_gate * sigmoid_gate).astype(jnp.bfloat16)
    grad_part = (contract_last(grad_gate, gate_mat) + contract_last(grad_up, up_mat)).astype(
        jnp.bfloat16
    )
    grad_returned = from_experts(grad_part, tp_size, ep_size, cap_src)
    grad_normed = jnp.sum(
        contract_first(placement, grad_returned).reshape(tok_dev, top_k, half_dim), axis=1
    )
    scaled = grad_normed * gain
    mean_partial = jnp.sum(tokens_f * scaled, axis=1, keepdims=True)
    grad_weights, mean_total = lax.psum((weight_partial, mean_partial), "section")
    grad_tokens = (inv_rms * scaled - tokens_f * inv_rms**3 * (mean_total / full_dim)).astype(
        jnp.bfloat16
    )
    return (routed, grad_tokens, grad_weights)


def solution(mesh):
    return jax.shard_map(
        local,
        mesh=mesh,
        in_specs=(
            P(("tp", "ep"), "section"),
            P("section"),
            P(("tp", "ep"), None),
            P(("tp", "ep"), None),
            P(("tp", "ep"), "section", None),
            P(("tp", "ep"), "section", None),
            P(("tp", "ep"), None, "section"),
            P(("tp", "ep"), "section"),
        ),
        out_specs=(P(("tp", "ep"), "section"), P(("tp", "ep"), "section"), P(("tp", "ep"), None)),
        check_vma=False,
    )
```

profile of v0, /device:TPU:2, one launch (start us, length us, event | category | flops | bytes accessed | tf_op | source)
XLA Modules:
  0.0 309.3 jit_solution(7530044829978923214)
XLA Ops:
  9.6 4.9 %psum.35 = f32[32,1]{0,1:T(1,128)S(1)} all-reduce(f32[32,1]{0,1:T(1,128)S(1)} %bitcast.48), channel_id=1, replica_groups=mesh['section'=2,'tp'=4,'ep'=32] {'section'}, use_global_device_ids=true, to_apply=%region_4.5 | all-reduce | flops 32 | bytes 256 | tf_op jit(solution)/shard_map/psum | solution.py:48
  16.6 1.4 reshape.106
  18.0 16.1 %all-to-all-start = ((bf16[128,2,2560]{2,1,0:T(2,128)(2,1)}), bf16[128,2,2560]{2,1,0:T(2,128)(2,1)}, u32[]{:S(2)}, u32[]{:S(2)}) async-start(bf16[128,2,2560]{2,1,0:T(2,128)(2,1)} %reshape.106), calls=%async_computation | async-start | bytes 2621440 | tf_op jit(solution)/shard_map/all_to_all | solution.py:24
  34.4 1.4 mul.141
  36.0 2.1 convolution_convert_fusion
  38.2 1.4 reshape.110
  39.5 30.2 %all-to-all-done = bf16[128,2,2560]{2,1,0:T(2,128)(2,1)} async-done(((bf16[128,2,2560]{2,1,0:T(2,128)(2,1)}), bf16[128,2,2560]{2,1,0:T(2,128)(2,1)}, u32[]{:S(2)}, u32[]{:S(2)}) %all-to-all-start) | async-done | bytes 1310752 | tf_op jit(solution)/shard_map/all_to_all | solution.py:24
  69.7 7.7 %all-to-all-start.2 = ((bf16[128,2,2560]{2,1,0:T(2,128)(2,1)}), bf16[128,2,2560]{2,1,0:T(2,128)(2,1)S(1)}, u32[]{:S(2)}, u32[]{:S(2)}) async-start(bf16[128,2,2560]{2,1,0:T(2,128)(2,1)} %reshape.110), calls=%async_computation.2 | async-start | bytes 2621440 | tf_op jit(solution)/shard_map/all_to_all | solution.py:24
  77.7 3.2 %reshape.107 = bf16[256,2560]{1,0:T(8,128)(2,1)S(1)} reshape(bf16[128,2,2560]{2,1,0:T(2,128)(2,1)} %all-to-all-done) | data formatting | bytes 2621440 | tf_op jit(solution)/shard_map/reshape | solution.py:25
  80.9 3.4 %fusion.5 = f32[256,768]{1,0:T(8,128)S(1)} fusion(bf16[256,2560]{1,0:T(8,128)(2,1)S(1)} %reshape.107, bf16[1,2560,768]{2,1,0:T(8,128)(2,1)} %param.13), kind=kOutput, calls=%fused_computation.6 | convolution fusion | flops 1006632960 | bytes 6029312 | tf_op jit(solution)/shard_map/dot_general | solution.py:68
  86.8 26.5 %all-to-all-done.2 = bf16[128,2,2560]{2,1,0:T(2,128)(2,1)S(1)} async-done(((bf16[128,2,2560]{2,1,0:T(2,128)(2,1)}), bf16[128,2,2560]{2,1,0:T(2,128)(2,1)S(1)}, u32[]{:S(2)}, u32[]{:S(2)}) %all-to-all-start.2) | async-done | bytes 1310752 | tf_op jit(solution)/shard_map/all_to_all | solution.py:24
  113.9 4.2 %fusion = f32[256,768]{1,0:T(8,128)} fusion(bf16[256,2560]{1,0:T(8,128)(2,1)S(1)} %reshape.111, bf16[1,768,2560]{2,1,0:T(8,128)(2,1)} %param.14), kind=kOutput, calls=%fused_computation.1 | convolution fusion | flops 1006632960 | bytes 6029312 | tf_op jit(solution)/shard_map/dot_general | solution.py:10
  118.1 75.8 %all-reduce.5.cloned.1.call-done = (f32[256,1536]{1,0:T(8,128)}, f32[256,768]{1,0:T(8,128)}) async-done(((f32[256,1536]{1,0:T(8,128)}, f32[256,768]{1,0:T(8,128)}), (f32[256,1536]{1,0:T(8,128)}, f32[256,768]{1,0:T(8,128)})) %all-reduce.5.cloned.1.call-update) | async-done | bytes 2359312 | tf_op jit(solution)/shard_map/psum | solution.py:72
  194.0 4.3 %fusion.7 = f32[256,2560]{1,0:T(8,128)S(1)} fusion(bf16[1,2560,768]{2,1,0:T(8,128)(2,1)} %param.12, f32[256,768]{1,0:T(8,128)} %get-tuple-element.8, f32[256,1536]{1,0:T(8,128)} %get-tuple-element.7), kind=kOutput, calls=%fused_computation.8 | convolution fusion | flops 1008599040 | bytes 8912896 | tf_op jit(solution)/shard_map/dot_general | solution.py:10
  199.9 1.4 reshape.112
  201.2 13.6 %all-to-all-start.3 = ((bf16[128,2,2560]{2,1,0:T(2,128)(2,1)}), bf16[128,2,2560]{2,1,0:T(2,128)(2,1)S(1)}, u32[]{:S(2)}, u32[]{:S(2)}) async-start(bf16[128,2,2560]{2,1,0:T(2,128)(2,1)} %reshape.112), calls=%async_computation.3 | async-start | bytes 2621440 | tf_op jit(solution)/shard_map/all_to_all | solution.py:31
  214.8 3.8 %fusion.11 = bf16[256,2560]{1,0:T(8,128)(2,1)S(1)} fusion(bf16[1,768,2560]{2,1,0:T(8,128)(2,1)} %param.14, f32[256,1536]{1,0:T(8,128)} %get-tuple-element.7), kind=kOutput, calls=%fused_computation.12 | convolution fusion | flops 1008467968 | bytes 6815744 | tf_op jit(solution)/shard_map/dot_general | solution.py:77
  218.6 1.4 reshape.108
  220.0 30.8 %all-to-all-done.3 = bf16[128,2,2560]{2,1,0:T(2,128)(2,1)S(1)} async-done(((bf16[128,2,2560]{2,1,0:T(2,128)(2,1)}), bf16[128,2,2560]{2,1,0:T(2,128)(2,1)S(1)}, u32[]{:S(2)}, u32[]{:S(2)}) %all-to-all-start.3) | async-done | bytes 1310752 | tf_op jit(solution)/shard_map/all_to_all | solution.py:31
  250.8 7.7 %all-to-all-start.1 = ((bf16[128,2,2560]{2,1,0:T(2,128)(2,1)}), bf16[128,2,2560]{2,1,0:T(2,128)(2,1)S(1)}, u32[]{:S(2)}, u32[]{:S(2)}) async-start(bf16[128,2,2560]{2,1,0:T(2,128)(2,1)} %reshape.108), calls=%async_computation.1 | async-start | bytes 2621440 | tf_op jit(solution)/shard_map/all_to_all | solution.py:31
  258.7 1.4 reshape.116
  260.0 1.8 convolution_reduce_fusion
  262.0 32.4 %all-to-all-done.1 = bf16[128,2,2560]{2,1,0:T(2,128)(2,1)S(1)} async-done(((bf16[128,2,2560]{2,1,0:T(2,128)(2,1)}), bf16[128,2,2560]{2,1,0:T(2,128)(2,1)S(1)}, u32[]{:S(2)}, u32[]{:S(2)}) %all-to-all-start.1) | async-done | bytes 1310752 | tf_op jit(solution)/shard_map/all_to_all | solution.py:31
  296.1 5.6 %all-reduce.1 = (f32[32,1]{0,1:T(1,128)S(1)}, f32[32,6]{0,1:T(8,128)}) all-reduce(f32[32,1]{0,1:T(1,128)S(1)} %bitcast.47, f32[32,6]{0,1:T(8,128)S(1)} %get-tuple-element.3), channel_id=1, replica_groups=mesh['section'=2,'tp'=4,'ep'=32] {'section'}, use_global_device_ids=true, to_apply=%region_10.11 | all-reduce | flops 224 | bytes 1792 | tf_op jit(solution)/shard_map/psum | solution.py:108
  (52 shorter events, 12.6 us)
Async XLA Ops:
  18.0 16.1 %copy-start.1 = (bf16[32,2560]{1,0:T(8,128)(2,1)S(1)}, bf16[32,2560]{1,0:T(8,128)(2,1)}, u32[]{:S(2)}) copy-start(bf16[32,2560]{1,0:T(8,128)(2,1)} %param.15) | copy-start | bytes 491524
  18.0 51.7 %all-to-all-start = ((bf16[128,2,2560]{2,1,0:T(2,128)(2,1)}), bf16[128,2,2560]{2,1,0:T(2,128)(2,1)}, u32[]{:S(2)}, u32[]{:S(2)}) async-start(bf16[128,2,2560]{2,1,0:T(2,128)(2,1)} %reshape.106), calls=%async_computation | async-start | bytes 2621440 | tf_op jit(solution)/shard_map/all_to_all | solution.py:24
  34.4 1.5 copy-start.3
  69.7 43.6 %all-to-all-start.2 = ((bf16[128,2,2560]{2,1,0:T(2,128)(2,1)}), bf16[128,2,2560]{2,1,0:T(2,128)(2,1)S(1)}, u32[]{:S(2)}, u32[]{:S(2)}) async-start(bf16[128,2,2560]{2,1,0:T(2,128)(2,1)} %reshape.110), calls=%async_computation.2 | async-start | bytes 2621440 | tf_op jit(solution)/shard_map/all_to_all | solution.py:24
  77.4 116.5 %all-reduce.5.cloned.1.call-start = ((), (), s32[]{:S(2)}) async-start(), calls=%async_computation.4 | async-start | bytes 4718592 | tf_op jit(solution)/shard_map/psum | solution.py:72
  80.8 3.5 %copy-start.4 = (bf16[1,2560,768]{2,1,0:T(8,128)(2,1)S(1)}, bf16[1,2560,768]{2,1,0:T(8,128)(2,1)}, u32[]{:S(2)}) copy-start(bf16[1,2560,768]{2,1,0:T(8,128)(2,1)} %param.12) | copy-start | bytes 11796484
  194.0 4.3 %copy-start.5 = (bf16[1,2560,768]{2,1,0:T(8,128)(2,1)S(1)}, bf16[1,2560,768]{2,1,0:T(8,128)(2,1)}, u32[]{:S(2)}) copy-start(bf16[1,2560,768]{2,1,0:T(8,128)(2,1)} %param.13) | copy-start | bytes 11796484
  194.0 4.4 %copy-start.6 = (f32[256,1536]{1,0:T(8,128)S(1)}, f32[256,1536]{1,0:T(8,128)}, u32[]{:S(2)}) copy-start(f32[256,1536]{1,0:T(8,128)} %get-tuple-element.7) | copy-start | bytes 4718596
  194.0 4.6 %copy-start.7 = (f32[256,768]{1,0:T(8,128)S(1)}, f32[256,768]{1,0:T(8,128)}, u32[]{:S(2)}) copy-start(f32[256,768]{1,0:T(8,128)} %get-tuple-element.8) | copy-start | bytes 2359300
  201.2 49.5 %all-to-all-start.3 = ((bf16[128,2,2560]{2,1,0:T(2,128)(2,1)}), bf16[128,2,2560]{2,1,0:T(2,128)(2,1)S(1)}, u32[]{:S(2)}, u32[]{:S(2)}) async-start(bf16[128,2,2560]{2,1,0:T(2,128)(2,1)} %reshape.112), calls=%async_computation.3 | async-start | bytes 2621440 | tf_op jit(solution)/shard_map/all_to_all | solution.py:31
  250.8 43.6 %all-to-all-start.1 = ((bf16[128,2,2560]{2,1,0:T(2,128)(2,1)}), bf16[128,2,2560]{2,1,0:T(2,128)(2,1)S(1)}, u32[]{:S(2)}, u32[]{:S(2)}) async-start(bf16[128,2,2560]{2,1,0:T(2,128)(2,1)} %reshape.108), calls=%async_computation.1 | async-start | bytes 2621440 | tf_op jit(solution)/shard_map/all_to_all | solution.py:31
  258.6 3.2 %copy-start = (bf16[32,2560]{1,0:T(8,128)(2,1)S(1)}, bf16[32,2560]{1,0:T(8,128)(2,1)}, u32[]{:S(2)}) copy-start(bf16[32,2560]{1,0:T(8,128)(2,1)} %param.8) | copy-start | bytes 491524
  258.7 3.2 %copy-start.2 = (f32[2560]{0:T(1024)S(1)}, f32[2560]{0:T(1024)}, u32[]{:S(2)}) copy-start(f32[2560]{0:T(1024)} %param.9) | copy-start | bytes 30724
Sparse Core Ops, SparseCore 0:
  118.3 75.6 all-reduce.4
where the time goes:
time: 310 us; the launch traced here: 309 us
  waiting for transfers between devices  196 us (63%)
  starting transfers between devices  45.2 us (15%)
  matrix products  23.7 us (8%)
  local copies, waits for them, and re-layouts  14.8 us (5%)
  between operations  14.3 us (5%)
  blocking collectives  10.5 us (3%)
  other arithmetic  4.98 us (2%)
    psum x1, waiting for transfers between devices, local(): joined = lax.psum(partial_pre, 'section')  75.8 us
    all_to_all x2, waiting for transfers between devices, from_experts(): lax.all_to_all(blocked, ('tp', 'ep'), split_axis=0, concat_axis=0, tiled=...  63.2 us
    all_to_all x2, waiting for transfers between devices, to_experts(): lax.all_to_all(blocked, ('tp', 'ep'), split_axis=0, concat_axis=0, tiled=...  56.7 us
    all_to_all x2, starting transfers between devices, to_experts(): lax.all_to_all(blocked, ('tp', 'ep'), split_axis=0, concat_axis=0, tiled=...  23.7 us
    all_to_all x2, starting transfers between devices, from_experts(): lax.all_to_all(blocked, ('tp', 'ep'), split_axis=0, concat_axis=0, tiled=...  21.3 us
    dot_general x3, matrix products, contract_last(): lax.dot_general(left, right, (((1,), (1,)), ((), ())), preferred_element_...  9.74 us
  transfers between devices with their start and end apart: 5, of which 5 were waited for; matrix products, arithmetic and copies ran while one was open for 8% of the time, Pallas kernels for 0%

commit v1 on v0

v1 whole, which is shorter than its diff:
```python
import jax
import jax.numpy as jnp
from jax import lax
from jax.sharding import PartitionSpec as P

EPS = 1e-06
BF = jnp.bfloat16
F32 = jnp.float32


def contract_last(left, right):
    return lax.dot_general(left, right, (((1,), (1,)), ((), ())), preferred_element_type=F32)


def contract_first(left, right):
    return lax.dot_general(left, right, (((0,), (0,)), ((), ())), preferred_element_type=F32)


def rounded(value):
    return lax.reduce_precision(value, exponent_bits=8, mantissa_bits=7)


def pieces(value):
    high = rounded(value)
    middle = rounded(value - high)
    return high, middle, value - high - middle


def packed(columns):
    rows = columns[0].shape[0]
    parts = [piece for column in columns for piece in pieces(column)]
    lane = lax.broadcasted_iota(jnp.int32, (rows, 128), 1)
    result = jnp.zeros((rows, 128), F32)
    for at, part in enumerate(parts):
        result = jnp.where(lane == at, part, result)
    return result.astype(BF)


def unpacked(block, at):
    block = block.astype(F32)
    return block[:, 3 * at : 3 * at + 1] + block[:, 3 * at + 1 : 3 * at + 2] + block[:, 3 * at + 2 : 3 * at + 3]


def exchange(rows, devices, cap_src):
    blocked = rows.reshape(devices, cap_src, rows.shape[1])
    moved = lax.all_to_all(blocked, ("tp", "ep"), split_axis=0, concat_axis=0, tiled=True)
    return moved.reshape(rows.shape)


def local(tokens, gain, routes, route_weights, w_gate, w_up, w_down, grad_out):
    tok_dev, half_dim = tokens.shape
    top_k = routes.shape[1]
    section_size = lax.axis_size("section")
    full_dim = half_dim * section_size
    experts = lax.axis_size("tp") * lax.axis_size("ep")
    cap_src = max(2, tok_dev * top_k // experts + 1)
    slots = experts * cap_src
    gate_mat, up_mat, down_mat = (w_gate[0], w_up[0], w_down[0])
    ff_dim = gate_mat.shape[1]
    swap = [(i, (i + 1) % section_size) for i in range(section_size)]

    routes_t = routes.T
    weights_t = route_weights.T
    slot = lax.broadcasted_iota(jnp.int32, (slots, tok_dev), 0)
    expert_of, rank_of = slot // cap_src, slot % cap_src
    named = [routes_t[k : k + 1, :] == expert_of for k in range(top_k)]
    member = sum(n.astype(F32) for n in named)
    earlier = lax.broadcasted_iota(jnp.int32, (tok_dev, tok_dev), 0) < lax.broadcasted_iota(
        jnp.int32, (tok_dev, tok_dev), 1
    )
    rank = jnp.dot(member.astype(BF), earlier.astype(BF), preferred_element_type=F32)
    at_rank = rank == rank_of.astype(F32)
    picked = jnp.where(at_rank, member, 0.0)
    select = picked.astype(BF)
    weighted = sum(
        jnp.where(named[k] & at_rank, weights_t[k : k + 1, :], 0.0) for k in range(top_k)
    )
    slot_weight = jnp.sum(weighted, axis=1, keepdims=True)

    outgoing = jnp.dot(select, tokens, preferred_element_type=F32).astype(BF)
    arrived = exchange(outgoing, experts, cap_src).astype(F32)
    grad_rows = (
        slot_weight * jnp.dot(select, grad_out, preferred_element_type=F32)
    ).astype(BF)
    grad_arrived = exchange(grad_rows, experts, cap_src)

    tokens_f = tokens.astype(F32)
    squares = jnp.sum(tokens_f * tokens_f, axis=1, keepdims=True)
    other_squares = lax.ppermute(squares, "section", swap)
    inv_rms = lax.rsqrt((squares + other_squares) / full_dim + EPS)

    scaled_rows = (arrived * gain).astype(BF)
    slot_squares = jnp.sum(arrived * arrived, axis=1, keepdims=True)
    own_pre = rounded(
        jnp.concatenate(
            [
                jnp.dot(scaled_rows, gate_mat, preferred_element_type=F32),
                jnp.dot(scaled_rows, up_mat, preferred_element_type=F32),
            ],
            axis=1,
        )
    )
    other_pre = lax.ppermute(
        jnp.concatenate([own_pre.astype(BF), packed([slot_squares])], axis=1), "section", swap
    )
    raw_pre = own_pre + other_pre[:, : 2 * ff_dim].astype(F32)
    slot_total = slot_squares + unpacked(other_pre[:, 2 * ff_dim :], 0)
    slot_inv = lax.rsqrt(slot_total / full_dim + EPS)
    raw_gate, raw_up = raw_pre[:, :ff_dim], raw_pre[:, ff_dim:]
    pre_gate, pre_up = raw_gate * slot_inv, raw_up * slot_inv
    sigmoid_gate = jax.nn.sigmoid(pre_gate)
    activated = (pre_gate * sigmoid_gate * pre_up).astype(BF)
    expert_out = jnp.dot(activated, down_mat, preferred_element_type=F32).astype(BF)
    returned = exchange(expert_out, experts, cap_src)

    own_act = rounded(contract_last(grad_arrived, down_mat))
    grad_act = own_act + lax.ppermute(own_act.astype(BF), "section", swap).astype(F32)
    grad_gate = (grad_act * pre_up * sigmoid_gate * (1.0 + pre_gate * (1.0 - sigmoid_gate))).astype(BF)
    grad_up = (grad_act * pre_gate * sigmoid_gate).astype(BF)
    weight_dot = jnp.sum(activated.astype(F32) * grad_act, axis=1, keepdims=True)
    mean_dot = jnp.sum(
        grad_gate.astype(F32) * raw_gate + grad_up.astype(F32) * raw_up, axis=1, keepdims=True
    )
    grad_part = (contract_last(grad_gate, gate_mat) + contract_last(grad_up, up_mat)).astype(BF)
    back = exchange(
        jnp.concatenate([grad_part, packed([weight_dot, mean_dot])], axis=1), experts, cap_src
    )

    weight_high = rounded(weighted)
    weight_low = weighted - weight_high
    halves = contract_first(
        jnp.concatenate([weight_high, weight_low], axis=1).astype(BF), returned
    )
    routed = (halves[:tok_dev] + halves[tok_dev:]).astype(BF)

    summed = contract_first(select, back)
    mean_total = unpacked(summed[:, half_dim:], 1)
    slot_dot = unpacked(back[:, half_dim:], 0)
    grad_weights = (
        jnp.stack(
            [
                jnp.sum(jnp.where(named[k] & at_rank, slot_dot, 0.0), axis=0)
                for k in range(top_k)
            ],
            axis=1,
        )
        / route_weights
    )
    scaled = summed[:, :half_dim] * gain
    grad_tokens = (inv_rms * scaled - tokens_f * inv_rms**3 * (mean_total / full_dim)).astype(BF)
    return (routed, grad_tokens, grad_weights)


def solution(mesh):
    return jax.shard_map(
        local,
        mesh=mesh,
        in_specs=(
            P(("tp", "ep"), "section"),
            P("section"),
            P(("tp", "ep"), None),
            P(("tp", "ep"), None),
            P(("tp", "ep"), "section", None),
            P(("tp", "ep"), "section", None),
            P(("tp", "ep"), None, "section"),
            P(("tp", "ep"), "section"),
        ),
        out_specs=(P(("tp", "ep"), "section"), P(("tp", "ep"), "section"), P(("tp", "ep"), None)),
        check_vma=False,
    )
```

time: 310 us -> 218 us (0.70)
  waiting for transfers between devices: 196 us -> 123 us
  between operations: 14.3 us -> 0.96 us
  blocking collectives: 10.5 us -> 0 us
  other arithmetic: 4.98 us -> 10.7 us
  matrix products: 23.7 us -> 20.1 us
    psum x1 -> x0, waiting for transfers between devices: 75.8 us -> none  [local(): joined = lax.psum(partial_pre, 'section')]
    psum x2 -> x0, blocking collectives: 10.5 us -> none  [the longest x1 5.55 us: local(): lax.psum((weight_partial, mean_partial), 'section')]
    ppermute x0 -> x3, waiting for transfers between devices: none -> 9.97 us  [the longest x1 6.15 us: local(): lax.ppermute(own_act.astype(BF), 'section', swap).astype(F32)]
    all_to_all x4, waiting for transfers between devices: 120 us -> 113 us  [exchange(): lax.all_to_all(blocked, ('tp', 'ep'), split_axis=0, concat_axis=0, tiled=...]
    convert_element_type x0 -> x2, local copies, waits for them, and re-layouts: none -> 4.17 us  [the longest x1 4.06 us: local(): scaled_rows = (arrived * gain).astype(BF)]
    reshape x10 -> x7, local copies, waits for them, and re-layouts: 11.6 us -> 8.78 us  [the longest x4 5.52 us: exchange(): blocked = rows.reshape(devices, cap_src, rows.shape[1])]
    dot_general x5 -> x6, matrix products: 11.1 us -> 9.55 us  [the longest x1 4.29 us: local(): jnp.dot(scaled_rows, up_mat, preferred_element_type=F32)]
  transfers between devices with their start and end apart: 5 -> 7, of which waited for: 5 -> 7; matrix products, arithmetic and copies ran while one was open for 8% -> 16% of each run, Pallas kernels for 0% -> 0%
where the time goes in v1:
time: 218 us; the launch traced here: 217 us
  waiting for transfers between devices  123 us (56%)
  starting transfers between devices  45.9 us (21%)
  matrix products  20.1 us (9%)
  local copies, waits for them, and re-layouts  16.6 us (8%)
  other arithmetic  10.7 us (5%)
    all_to_all x4, waiting for transfers between devices, exchange(): lax.all_to_all(blocked, ('tp', 'ep'), split_axis=0, concat_axis=0, tiled=...  113 us
    all_to_all x4, starting transfers between devices, exchange(): lax.all_to_all(blocked, ('tp', 'ep'), split_axis=0, concat_axis=0, tiled=...  44.2 us
    dot_general x3, matrix products, contract_last(): lax.dot_general(left, right, (((1,), (1,)), ((), ())), preferred_element_...  8.46 us
    ppermute x1, waiting for transfers between devices, local(): lax.ppermute(own_act.astype(BF), 'section', swap).astype(F32)  6.15 us
    reshape x4, local copies, waits for them, and re-layouts, exchange(): blocked = rows.reshape(devices, cap_src, rows.shape[1])  5.52 us
  transfers between devices with their start and end apart: 7, of which 7 were waited for; matrix products, arithmetic and copies ran while one was open for 16% of the time, Pallas kernels for 0%

profile of v1, /device:TPU:2, one launch (start us, length us, event | category | flops | bytes accessed | tf_op | source)
XLA Modules:
  0.0 217.3 jit_solution(2881553736930016102)
XLA Ops:
  2.8 1.5 convolution_convert_fusion
  4.3 1.4 reshape.97
  5.7 15.5 %all-to-all-start = ((bf16[128,2,2560]{2,1,0:T(2,128)(2,1)}), bf16[128,2,2560]{2,1,0:T(2,128)(2,1)S(1)}, u32[]{:S(2)}, u32[]{:S(2)}) async-start(bf16[128,2,2560]{2,1,0:T(2,128)(2,1)} %reshape.97), calls=%async_computation | async-start | bytes 2621440 | tf_op jit(solution)/shard_map/all_to_all | solution.py:46
  21.9 1.4 reshape.100
  23.3 33.9 %all-to-all-done = bf16[128,2,2560]{2,1,0:T(2,128)(2,1)S(1)} async-done(((bf16[128,2,2560]{2,1,0:T(2,128)(2,1)}), bf16[128,2,2560]{2,1,0:T(2,128)(2,1)S(1)}, u32[]{:S(2)}, u32[]{:S(2)}) %all-to-all-start) | async-done | bytes 1310752 | tf_op jit(solution)/shard_map/all_to_all | solution.py:46
  57.2 7.7 %all-to-all-start.2 = ((bf16[128,2,2560]{2,1,0:T(2,128)(2,1)}), bf16[128,2,2560]{2,1,0:T(2,128)(2,1)S(1)}, u32[]{:S(2)}, u32[]{:S(2)}) async-start(bf16[128,2,2560]{2,1,0:T(2,128)(2,1)} %reshape.100), calls=%async_computation.2 | async-start | bytes 2621440 | tf_op jit(solution)/shard_map/all_to_all | solution.py:46
  64.9 3.2 %fusion.19 = (f32[128,2]{1,0:T(8,128)S(1)}, bf16[128,2,2560]{2,1,0:T(2,128)(2,1)}) fusion(bf16[128,2,2560]{2,1,0:T(2,128)(2,1)S(1)} %all-to-all-done, f32[2560]{0:T(1024)S(1)} %copy-done.5), kind=kLoop, calls=%fused_computation.20 | loop fusion | flops 3276544 | bytes 2632704 | tf_op jit(solution)/shard_map/reduce_sum | solution.py:93
  68.1 4.1 %convert_element_type.117 = bf16[256,2560]{1,0:T(8,128)(2,1)} reshape(bf16[128,2,2560]{2,1,0:T(2,128)(2,1)} %get-tuple-element.21) | data formatting | bytes 2621440 | tf_op jit(solution)/shard_map/convert_element_type | solution.py:92
  72.5 4.3 %fusion.5 = f32[256,768]{0,1:T(8,128)S(1)} fusion(bf16[256,2560]{1,0:T(8,128)(2,1)} %convert_element_type.117, bf16[1,2560,768]{2,1,0:T(8,128)(2,1)} %param.13), kind=kOutput, calls=%fused_computation.7 | convolution fusion | flops 1006632960 | bytes 6029312 | tf_op jit(solution)/shard_map/dot_general | solution.py:98
  76.8 1.6 fusion.9
  80.4 20.5 %all-to-all-done.2 = bf16[128,2,2560]{2,1,0:T(2,128)(2,1)S(1)} async-done(((bf16[128,2,2560]{2,1,0:T(2,128)(2,1)}), bf16[128,2,2560]{2,1,0:T(2,128)(2,1)S(1)}, u32[]{:S(2)}, u32[]{:S(2)}) %all-to-all-start.2) | async-done | bytes 1310752 | tf_op jit(solution)/shard_map/all_to_all | solution.py:46
  102.2 3.7 %fusion.65 = (bf16[256,768]{0,1:T(8,128)(2,1)S(1)}, f32[256,768]{0,1:T(8,128)S(1)}) fusion(bf16[256,2560]{1,0:T(8,128)(2,1)} %reshape.101, bf16[1,768,2560]{2,1,0:T(8,128)(2,1)} %param.14), kind=kOutput, calls=%fused_computation.141 | convolution fusion | flops 1007026176 | bytes 6422528 | tf_op jit(solution)/shard_map/dot_general | solution.py:12
  109.1 6.2 %collective-permute-done.2 = bf16[256,768]{0,1:T(8,128)(2,1)S(1)} collective-permute-done((bf16[256,768]{0,1:T(8,128)(2,1)S(1)}, bf16[256,768]{0,1:T(8,128)(2,1)S(1)}, u32[]{:S(2)}, u32[]{:S(2)}) %collective-permute-start.2) | collective-permute-done | bytes 393248 | tf_op jit(solution)/shard_map/ppermute | solution.py:117
  115.9 1.4 copy-done.7
  118.6 1.4 reshape.98
  119.9 13.3 %all-to-all-start.1 = ((bf16[128,2,2560]{2,1,0:T(2,128)(2,1)}), bf16[128,2,2560]{2,1,0:T(2,128)(2,1)S(1)}, u32[]{:S(2)}, u32[]{:S(2)}) async-start(bf16[128,2,2560]{2,1,0:T(2,128)(2,1)} %reshape.98), calls=%async_computation.1 | async-start | bytes 2621440 | tf_op jit(solution)/shard_map/all_to_all | solution.py:46
  133.6 3.5 %fusion.7 = f32[256,2560]{1,0:T(8,128)S(1)} fusion(bf16[256,768]{0,1:T(8,128)(2,1)S(1)} %get-tuple-element.12, bf16[1,2560,768]{2,1,0:T(8,128)(2,1)} %param.12), kind=kOutput, calls=%fused_computation.9 | convolution fusion | flops 1006632960 | bytes 6946816 | tf_op jit(solution)/shard_map/dot_general | solution.py:12
  138.5 1.4 reshape.102
  139.9 29.3 %all-to-all-done.1 = bf16[128,2,2560]{2,1,0:T(2,128)(2,1)S(1)} async-done(((bf16[128,2,2560]{2,1,0:T(2,128)(2,1)}), bf16[128,2,2560]{2,1,0:T(2,128)(2,1)S(1)}, u32[]{:S(2)}, u32[]{:S(2)}) %all-to-all-start.1) | async-done | bytes 1310752 | tf_op jit(solution)/shard_map/all_to_all | solution.py:46
  169.2 7.7 %all-to-all-start.3 = ((bf16[128,2,2688]{2,1,0:T(2,128)(2,1)}), bf16[128,2,2688]{2,1,0:T(2,128)(2,1)S(1)}, u32[]{:S(2)}, u32[]{:S(2)}) async-start(bf16[128,2,2688]{2,1,0:T(2,128)(2,1)} %reshape.102), calls=%async_computation.3 | async-start | bytes 2752512 | tf_op jit(solution)/shard_map/all_to_all | solution.py:46
  177.4 3.6 %collective-permute-done.1 = f32[32,1]{1,0:T(8,128)S(1)} collective-permute-done((f32[32,1]{1,0:T(8,128)S(1)}, f32[32,1]{1,0:T(8,128)S(1)}, u32[]{:S(2)}, u32[]{:S(2)}) %collective-permute-start.1) | collective-permute-done | bytes 160 | tf_op jit(solution)/shard_map/ppermute | solution.py:89
  181.2 1.4 reshape.99
  182.6 1.7 fusion.49
  184.9 29.3 %all-to-all-done.3 = bf16[128,2,2688]{2,1,0:T(2,128)(2,1)S(1)} async-done(((bf16[128,2,2688]{2,1,0:T(2,128)(2,1)}), bf16[128,2,2688]{2,1,0:T(2,128)(2,1)S(1)}, u32[]{:S(2)}, u32[]{:S(2)}) %all-to-all-start.3) | async-done | bytes 1376288 | tf_op jit(solution)/shard_map/all_to_all | solution.py:46
  (62 shorter events, 17.3 us)
Async XLA Ops:
  0.6 20.6 %copy-start = (bf16[32,2560]{1,0:T(8,128)(2,1)S(1)}, bf16[32,2560]{1,0:T(8,128)(2,1)}, u32[]{:S(2)}) copy-start(bf16[32,2560]{1,0:T(8,128)(2,1)} %param.15) | copy-start | bytes 491524
  5.7 51.5 %all-to-all-start = ((bf16[128,2,2560]{2,1,0:T(2,128)(2,1)}), bf16[128,2,2560]{2,1,0:T(2,128)(2,1)S(1)}, u32[]{:S(2)}, u32[]{:S(2)}) async-start(bf16[128,2,2560]{2,1,0:T(2,128)(2,1)} %reshape.97), calls=%async_computation | async-start | bytes 2621440 | tf_op jit(solution)/shard_map/all_to_all | solution.py:46
  23.2 41.6 %copy-start.5 = (f32[2560]{0:T(1024)S(1)}, f32[2560]{0:T(1024)}, u32[]{:S(2)}) copy-start(f32[2560]{0:T(1024)} %param.9) | copy-start | bytes 30724
  57.2 43.7 %all-to-all-start.2 = ((bf16[128,2,2560]{2,1,0:T(2,128)(2,1)}), bf16[128,2,2560]{2,1,0:T(2,128)(2,1)S(1)}, u32[]{:S(2)}, u32[]{:S(2)}) async-start(bf16[128,2,2560]{2,1,0:T(2,128)(2,1)} %reshape.100), calls=%async_computation.2 | async-start | bytes 2621440 | tf_op jit(solution)/shard_map/all_to_all | solution.py:46
  72.5 4.3 %copy-start.1 = (bf16[1,2560,768]{2,1,0:T(8,128)(2,1)S(1)}, bf16[1,2560,768]{2,1,0:T(8,128)(2,1)}, u32[]{:S(2)}) copy-start(bf16[1,2560,768]{2,1,0:T(8,128)(2,1)} %param.12) | copy-start | bytes 11796484
  72.5 4.3 %copy-start.4 = (bf16[256,2560]{1,0:T(8,128)(2,1)S(1)}, bf16[256,2560]{1,0:T(8,128)(2,1)}, u32[]{:S(2)}) copy-start(bf16[256,2560]{1,0:T(8,128)(2,1)} %convert_element_type.117) | copy-start | bytes 3932164
  79.5 27.4 %collective-permute-start = (bf16[256,1664]{0,1:T(8,128)(2,1)}, bf16[256,1664]{0,1:T(8,128)(2,1)}, u32[]{:S(2)}, u32[]{:S(2)}) collective-permute-start(bf16[256,1664]{0,1:T(8,128)(2,1)} %pad_maximum_fusion.1), channel_id=1, source_target_pairs={{0,128},{128,0},{1,129},{129,1},{2,130},{130,2},{3,131},{131,3},{4... | collective-permute-start | bytes 2555912 | tf_op jit(solution)/shard_map/ppermute | solution.py:103
  106.0 9.3 %collective-permute-start.2 = (bf16[256,768]{0,1:T(8,128)(2,1)S(1)}, bf16[256,768]{0,1:T(8,128)(2,1)S(1)}, u32[]{:S(2)}, u32[]{:S(2)}) collective-permute-start(bf16[256,768]{0,1:T(8,128)(2,1)S(1)} %get-tuple-element.46), channel_id=1, source_target_pairs={{0,128},{128,0},{1,129},{129,1},{2,130},{130,2},{3,131},{131,3},{4... | collective-permute-start | bytes 1179656 | tf_op jit(solution)/shard_map/ppermute | solution.py:117
  115.2 2.1 copy-start.7
  119.9 49.3 %all-to-all-start.1 = ((bf16[128,2,2560]{2,1,0:T(2,128)(2,1)}), bf16[128,2,2560]{2,1,0:T(2,128)(2,1)S(1)}, u32[]{:S(2)}, u32[]{:S(2)}) async-start(bf16[128,2,2560]{2,1,0:T(2,128)(2,1)} %reshape.98), calls=%async_computation.1 | async-start | bytes 2621440 | tf_op jit(solution)/shard_map/all_to_all | solution.py:46
  133.6 3.5 %copy-start.2 = (bf16[1,2560,768]{2,1,0:T(8,128)(2,1)S(1)}, bf16[1,2560,768]{2,1,0:T(8,128)(2,1)}, u32[]{:S(2)}) copy-start(bf16[1,2560,768]{2,1,0:T(8,128)(2,1)} %param.13) | copy-start | bytes 11796484
  139.9 37.0 %copy-start.3 = (bf16[32,2560]{1,0:T(8,128)(2,1)S(1)}, bf16[32,2560]{1,0:T(8,128)(2,1)}, u32[]{:S(2)}) copy-start(bf16[32,2560]{1,0:T(8,128)(2,1)} %param.8) | copy-start | bytes 491524
  169.2 45.0 %all-to-all-start.3 = ((bf16[128,2,2688]{2,1,0:T(2,128)(2,1)}), bf16[128,2,2688]{2,1,0:T(2,128)(2,1)S(1)}, u32[]{:S(2)}, u32[]{:S(2)}) async-start(bf16[128,2,2688]{2,1,0:T(2,128)(2,1)} %reshape.102), calls=%async_computation.3 | async-start | bytes 2752512 | tf_op jit(solution)/shard_map/all_to_all | solution.py:46
  177.2 3.9 %collective-permute-start.1 = (f32[32,1]{1,0:T(8,128)S(1)}, f32[32,1]{1,0:T(8,128)S(1)}, u32[]{:S(2)}, u32[]{:S(2)}) collective-permute-start(f32[32,1]{1,0:T(8,128)S(1)} %copy.23), channel_id=1, source_target_pairs={{0,128},{128,0},{1,129},{129,1},{2,130},{130,2},{3,131},{131,3},{4... | collective-permute-start | bytes 392 | tf_op jit(solution)/shard_map/ppermute | solution.py:89
  214.7 1.1 copy-start.6

commit v2 on v1

v2 whole, which is shorter than its diff:
```python
import jax
import jax.numpy as jnp
from jax import lax
from jax.experimental import pallas as pl
from jax.experimental.pallas import tpu as pltpu
from jax.sharding import PartitionSpec as P

EPS = 1e-06
BF = jnp.bfloat16
F32 = jnp.float32


def contract_last(left, right):
    return lax.dot_general(left, right, (((1,), (1,)), ((), ())), preferred_element_type=F32)


def contract_first(left, right):
    return lax.dot_general(left, right, (((0,), (0,)), ((), ())), preferred_element_type=F32)


SMALL = pl.CostEstimate(flops=1, bytes_accessed=1, transcendentals=0)
ROOM = pltpu.CompilerParams(vmem_limit_bytes=40 * 1024 * 1024)


def act_kernel(rows_ref, down_ref, out_ref):
    out_ref[...] = contract_last(rows_ref[...], down_ref[...]).astype(BF)


def grad_act_part(rows, down_mat):
    slots, half_dim = rows.shape
    ff_dim = down_mat.shape[0]
    block = 256
    return pl.pallas_call(
        act_kernel,
        grid=(ff_dim // block,),
        in_specs=[
            pl.BlockSpec((slots, half_dim), lambda i: (0, 0)),
            pl.BlockSpec((block, half_dim), lambda i: (i, 0)),
        ],
        out_specs=pl.BlockSpec((slots, block), lambda i: (0, i)),
        out_shape=jax.ShapeDtypeStruct((slots, ff_dim), BF),
        compiler_params=ROOM,
        cost_estimate=SMALL,
        name="grad_act",
    )(rows, down_mat)


def in_pieces(value):
    high = value.astype(BF).astype(F32)
    middle = (value - high).astype(BF).astype(F32)
    return high, middle, value - high - middle


def part_kernel(
    pre_a, pre_b, act_a, act_b, done_ref, gate_ref, up_ref, out_ref, gate_grad, up_grad
):
    ff_dim = act_a.shape[1]
    half_dim = done_ref.shape[1]
    block = gate_ref.shape[0]
    step = pl.program_id(0)

    @pl.when(step == 0)
    def _():
        pre_gate = pre_a[:, :ff_dim].astype(F32) + pre_b[:, :ff_dim].astype(F32)
        pre_up = pre_a[:, ff_dim:].astype(F32) + pre_b[:, ff_dim:].astype(F32)
        grad_act = act_a[...].astype(F32) + act_b[...].astype(F32)
        sigmoid_gate = jax.nn.sigmoid(pre_gate)
        activated = (pre_gate * sigmoid_gate * pre_up).astype(BF)
        by_gate = grad_act * pre_up * sigmoid_gate * (1.0 + pre_gate * (1.0 - sigmoid_gate))
        by_up = grad_act * pre_gate * sigmoid_gate
        gate_grad[...] = by_gate.astype(BF)
        up_grad[...] = by_up.astype(BF)
        weight_dot = jnp.sum(activated.astype(F32) * grad_act, axis=1, keepdims=True)
        mean_dot = jnp.sum(by_gate * pre_gate + by_up * pre_up, axis=1, keepdims=True)
        lane = lax.broadcasted_iota(jnp.int32, (done_ref.shape[0], 128), 1)
        sums = jnp.zeros(lane.shape, F32)
        for at, part in enumerate(in_pieces(weight_dot) + in_pieces(mean_dot)):
            sums = jnp.where(lane == at, part, sums)
        out_ref[:, 2 * half_dim :] = sums.astype(BF)
        out_ref[:, :half_dim] = done_ref[...]

    columns = pl.ds(pl.multiple_of(half_dim + step * block, 128), block)
    out_ref[:, columns] = (
        contract_last(gate_grad[...], gate_ref[...]) + contract_last(up_grad[...], up_ref[...])
    ).astype(BF)


def grad_parts(own_pre, other_pre, own_act, other_act, expert_out, gate_mat, up_mat):
    slots, ff_dim = own_act.shape
    half_dim = gate_mat.shape[0]
    block = 512
    whole = lambda width: pl.BlockSpec((slots, width), lambda i: (0, 0))
    weights = pl.BlockSpec((block, ff_dim), lambda i: (i, 0))
    return pl.pallas_call(
        part_kernel,
        grid=(half_dim // block,),
        in_specs=[whole(2 * ff_dim)] * 2 + [whole(ff_dim)] * 2 + [whole(half_dim)] + [weights] * 2,
        out_specs=whole(2 * half_dim + 128),
        out_shape=jax.ShapeDtypeStruct((slots, 2 * half_dim + 128), BF),
        scratch_shapes=[pltpu.VMEM((slots, ff_dim), BF)] * 2,
        compiler_params=ROOM,
        cost_estimate=SMALL,
        name="grad_parts",
    )(own_pre, other_pre, own_act, other_act, expert_out, gate_mat, up_mat)


def rounded(value):
    return lax.reduce_precision(value, exponent_bits=8, mantissa_bits=7)


def unpacked(block, at):
    block = block.astype(F32)
    return block[:, 3 * at : 3 * at + 1] + block[:, 3 * at + 1 : 3 * at + 2] + block[:, 3 * at + 2 : 3 * at + 3]


def blocks(rows, devices):
    return rows.reshape(devices, rows.shape[0] // devices, rows.shape[1])


def exchange(blocked):
    return lax.all_to_all(blocked, ("tp", "ep"), split_axis=0, concat_axis=0, tiled=True)


def local(tokens, gain, routes, route_weights, w_gate, w_up, w_down, grad_out):
    tok_dev, half_dim = tokens.shape
    top_k = routes.shape[1]
    section_size = lax.axis_size("section")
    full_dim = half_dim * section_size
    experts = lax.axis_size("tp") * lax.axis_size("ep")
    cap_src = max(2, tok_dev * top_k // experts + 1)
    slots = experts * cap_src
    gate_mat, up_mat, down_mat = (w_gate[0], w_up[0], w_down[0])
    ff_dim = gate_mat.shape[1]
    swap = [(i, (i + 1) % section_size) for i in range(section_size)]

    routes_t = routes.T
    weights_t = route_weights.T
    slot = lax.broadcasted_iota(jnp.int32, (slots, tok_dev), 0)
    expert_of, rank_of = slot // cap_src, slot % cap_src
    named = [routes_t[k : k + 1, :] == expert_of for k in range(top_k)]
    member = sum(n.astype(F32) for n in named)
    earlier = lax.broadcasted_iota(jnp.int32, (tok_dev, tok_dev), 0) < lax.broadcasted_iota(
        jnp.int32, (tok_dev, tok_dev), 1
    )
    rank = jnp.dot(member.astype(BF), earlier.astype(BF), preferred_element_type=F32)
    at_rank = rank == rank_of.astype(F32)
    picked = jnp.where(at_rank, member, 0.0)
    select = picked.astype(BF)
    weighted = sum(
        jnp.where(named[k] & at_rank, weights_t[k : k + 1, :], 0.0) for k in range(top_k)
    )
    slot_weight = jnp.sum(weighted, axis=1, keepdims=True)

    tokens_f = tokens.astype(F32)
    squares = jnp.sum(tokens_f * tokens_f, axis=1, keepdims=True)
    inv_rms = lax.rsqrt((squares + lax.ppermute(squares, "section", swap)) / full_dim + EPS)
    normed = (tokens_f * inv_rms * gain).astype(BF)
    outgoing = jnp.dot(select, normed, preferred_element_type=F32).astype(BF)
    arrived = exchange(blocks(outgoing, experts)).reshape(slots, half_dim)
    grad_rows = (
        slot_weight * jnp.dot(select, grad_out, preferred_element_type=F32)
    ).astype(BF)
    grad_blocks = exchange(blocks(grad_rows, experts))

    own_pre = rounded(
        jnp.concatenate(
            [
                jnp.dot(arrived, gate_mat, preferred_element_type=F32),
                jnp.dot(arrived, up_mat, preferred_element_type=F32),
            ],
            axis=1,
        )
    )
    pre_send = own_pre.astype(BF)
    other_pre = lax.ppermute(pre_send, "section", swap)
    pre = own_pre + other_pre.astype(F32)
    pre_gate, pre_up = pre[:, :ff_dim], pre[:, ff_dim:]
    sigmoid_gate = jax.nn.sigmoid(pre_gate)
    activated = lax.optimization_barrier((pre_gate * sigmoid_gate * pre_up).astype(BF))
    expert_out = jnp.dot(activated, down_mat, preferred_element_type=F32).astype(BF)
    grad_arrived = grad_blocks.reshape(slots, half_dim)
    own_act = grad_act_part(grad_arrived, down_mat)
    other_act = lax.ppermute(own_act, "section", swap)
    parts = grad_parts(pre_send, other_pre, own_act, other_act, expert_out, gate_mat, up_mat)
    back = exchange(blocks(parts, experts)).reshape(parts.shape)
    returned, back = back[:, :half_dim], back[:, half_dim:]

    weight_high = rounded(weighted)
    weight_low = weighted - weight_high
    halves = contract_first(
        jnp.concatenate([weight_high, weight_low], axis=1).astype(BF), returned
    )
    routed = (halves[:tok_dev] + halves[tok_dev:]).astype(BF)

    summed = contract_first(select, back)
    mean_total = unpacked(summed[:, half_dim:], 1) / inv_rms
    slot_dot = unpacked(back[:, half_dim:], 0)
    grad_weights = (
        jnp.stack(
            [
                jnp.sum(jnp.where(named[k] & at_rank, slot_dot, 0.0), axis=0)
                for k in range(top_k)
            ],
            axis=1,
        )
        / route_weights
    )
    scaled = summed[:, :half_dim] * gain
    grad_tokens = (inv_rms * scaled - tokens_f * inv_rms**3 * (mean_total / full_dim)).astype(BF)
    return (routed, grad_tokens, grad_weights)


def solution(mesh):
    return jax.shard_map(
        local,
        mesh=mesh,
        in_specs=(
            P(("tp", "ep"), "section"),
            P("section"),
            P(("tp", "ep"), None),
            P(("tp", "ep"), None),
            P(("tp", "ep"), "section", None),
            P(("tp", "ep"), "section", None),
            P(("tp", "ep"), None, "section"),
            P(("tp", "ep"), "section"),
        ),
        out_specs=(P(("tp", "ep"), "section"), P(("tp", "ep"), "section"), P(("tp", "ep"), None)),
        check_vma=False,
    )
```

time: 218 us -> 212 us (0.972)
  blocking collectives: 0 us -> 74.2 us
  waiting for transfers between devices: 123 us -> 69 us
  starting transfers between devices: 45.9 us -> 26.8 us
  matrix products: 20.1 us -> 8.96 us
  other arithmetic: 10.7 us -> 4.56 us
  Pallas kernels: 0 us -> 5.67 us
  local copies, waits for them, and re-layouts: 16.6 us -> 21 us
    all_to_all x0 -> x1, blocking collectives: none -> 74.2 us  [exchange(): lax.all_to_all(blocked, ('tp', 'ep'), split_axis=0, concat_axis=0, tiled=...]
    all_to_all x4 -> x2, waiting for transfers between devices: 113 us -> 62.9 us  [exchange(): lax.all_to_all(blocked, ('tp', 'ep'), split_axis=0, concat_axis=0, tiled=...]
    all_to_all x4 -> x2, starting transfers between devices: 44.2 us -> 23.6 us  [exchange(): lax.all_to_all(blocked, ('tp', 'ep'), split_axis=0, concat_axis=0, tiled=...]
    dot_general x6 -> x3, matrix products: 15.9 us -> 6.16 us  [the longest x1 3.44 us: local(): jnp.dot(arrived, up_mat, preferred_element_type=F32)]
    pallas_call x0 -> x2, Pallas kernels: none -> 5.67 us  [the longest x1 4.01 us: grad_parts(): pl.pallas_call(part_kernel, grid=(half_dim // block,), in_specs=[whole(2...]
    reshape x7 -> x6, local copies, waits for them, and re-layouts: 8.78 us -> 14.4 us  [the longest x1 5.41 us: local(): back = exchange(blocks(parts, experts)).reshape(parts.shape)]
    convert_element_type x2 -> x0, local copies, waits for them, and re-layouts: 4.17 us -> none  [the longest x1 4.06 us: local(): scaled_rows = (arrived * gain).astype(BF)]
    reduce_sum x2 -> x0, other arithmetic: 3.95 us -> none  [the longest x1 3.25 us: local(): slot_squares = jnp.sum(arrived * arrived, axis=1, keepdims=True)]
  transfers between devices with their start and end apart: 7 -> 5, of which waited for: 7 -> 3; matrix products, arithmetic and copies ran while one was open for 16% -> 7% of each run, Pallas kernels for 0% -> 1%
where the time goes in v2:
time: 212 us; the launch traced here: 211 us
  blocking collectives  74.2 us (35%)
  waiting for transfers between devices  69 us (33%)
  starting transfers between devices  26.8 us (13%)
  local copies, waits for them, and re-layouts  21 us (10%)
  matrix products  8.96 us (4%)
  Pallas kernels  5.67 us (3%)
  other arithmetic  4.56 us (2%)
    all_to_all x1, blocking collectives, exchange(): lax.all_to_all(blocked, ('tp', 'ep'), split_axis=0, concat_axis=0, tiled=...  74.2 us
    all_to_all x2, waiting for transfers between devices, exchange(): lax.all_to_all(blocked, ('tp', 'ep'), split_axis=0, concat_axis=0, tiled=...  62.9 us
    all_to_all x2, starting transfers between devices, exchange(): lax.all_to_all(blocked, ('tp', 'ep'), split_axis=0, concat_axis=0, tiled=...  23.6 us
    ppermute x1, waiting for transfers between devices, local(): other_act = lax.ppermute(own_act, 'section', swap)  6.15 us
    reshape x1, local copies, waits for them, and re-layouts, local(): back = exchange(blocks(parts, experts)).reshape(parts.shape)  5.41 us
    reshape x3, local copies, waits for them, and re-layouts, blocks(): return rows.reshape(devices, rows.shape[0] // devices, rows.shape[1])  5.25 us
    unnamed x32, local copies, waits for them, and re-layouts  4.72 us
  transfers between devices with their start and end apart: 5, of which 3 were waited for; matrix products, arithmetic and copies ran while one was open for 7% of the time, Pallas kernels for 1%

profile of v2, /device:TPU:2, one launch (start us, length us, event | category | flops | bytes accessed | tf_op | source)
XLA Modules:
  0.0 211.3 jit_solution(12968175023351237924)
XLA Ops:
  0.6 1.1 fusion.7
  1.8 1.6 collective-permute-start
  3.4 0.9 slice_bitcast_fusion.11
  4.4 0.9 slice_bitcast_fusion.5
  5.7 1.5 convolution_convert_fusion.1
  7.2 1.4 reshape.26
  8.6 15.5 %all-to-all-start = ((bf16[128,2,2560]{2,1,0:T(2,128)(2,1)}), bf16[128,2,2560]{2,1,0:T(2,128)(2,1)S(1)}, u32[]{:S(2)}, u32[]{:S(2)}) async-start(bf16[128,2,2560]{2,1,0:T(2,128)(2,1)} %reshape.26), calls=%async_computation | async-start | bytes 2621440 | tf_op jit(solution)/shard_map/all_to_all | solution.py:121
  24.8 1.4 reshape.28
  26.2 33.9 %all-to-all-done = bf16[128,2,2560]{2,1,0:T(2,128)(2,1)S(1)} async-done(((bf16[128,2,2560]{2,1,0:T(2,128)(2,1)}), bf16[128,2,2560]{2,1,0:T(2,128)(2,1)S(1)}, u32[]{:S(2)}, u32[]{:S(2)}) %all-to-all-start) | async-done | bytes 1310752 | tf_op jit(solution)/shard_map/all_to_all | solution.py:121
  60.1 8.1 %all-to-all-start.1 = ((bf16[128,2,2560]{2,1,0:T(2,128)(2,1)}), bf16[128,2,2560]{2,1,0:T(2,128)(2,1)}, u32[]{:S(2)}, u32[]{:S(2)}) async-start(bf16[128,2,2560]{2,1,0:T(2,128)(2,1)} %reshape.28), calls=%async_computation.1 | async-start | bytes 2621440 | tf_op jit(solution)/shard_map/all_to_all | solution.py:121
  68.7 3.4 %fusion.50 = f32[256,768]{1,0:T(8,128)S(1)} fusion(bf16[256,2560]{1,0:T(8,128)(2,1)S(1)} %reshape.27, bf16[1,2560,768]{2,1,0:T(8,128)(2,1)} %param.13), kind=kOutput, calls=%fused_computation.102 | convolution fusion | flops 1006632960 | bytes 6029312 | tf_op jit(solution)/shard_map/dot_general | solution.py:169
  72.2 1.2 fusion.52
  75.0 28.9 %all-to-all-done.1 = bf16[128,2,2560]{2,1,0:T(2,128)(2,1)} async-done(((bf16[128,2,2560]{2,1,0:T(2,128)(2,1)}), bf16[128,2,2560]{2,1,0:T(2,128)(2,1)}, u32[]{:S(2)}, u32[]{:S(2)}) %all-to-all-start.1) | async-done | bytes 1310752 | tf_op jit(solution)/shard_map/all_to_all | solution.py:121
  103.9 3.2 %reshape.29.rows_ref = bf16[256,2560]{1,0:T(8,128)(2,1)S(1)} reshape(bf16[128,2,2560]{2,1,0:T(2,128)(2,1)} %all-to-all-done.1) | data formatting | bytes 2621440 | tf_op jit(solution)/shard_map/reshape | solution.py:181
  107.1 2.1 copy-done.1
  109.2 1.7 grad_act.1.act_a
  110.9 0.9 collective-permute-start.2
  113.0 1.2 convolution_convert_fusion.done_ref
  114.2 6.2 %collective-permute-done.2.act_b = bf16[256,768]{1,0:T(8,128)(2,1)S(1)} collective-permute-done((bf16[256,768]{1,0:T(8,128)(2,1)S(1)}, bf16[256,768]{1,0:T(8,128)(2,1)S(1)}, u32[]{:S(2)}, u32[]{:S(2)}) %collective-permute-start.2) | collective-permute-done | bytes 393248 | tf_op jit(solution)/shard_map/ppermute | solution.py:183
  120.3 1.1 copy-done.8
  121.5 4.0 %grad_parts.1 = bf16[256,5248]{1,0:T(8,128)(2,1)S(1)} custom-call(bf16[256,1536]{1,0:T(8,128)(2,1)S(1)} %copy-done.6, bf16[256,1536]{1,0:T(8,128)(2,1)S(1)} %copy-done.8, bf16[256,768]{1,0:T(8,128)(2,1)S(1)} %grad_act.1.act_a, bf16[256,768]{1,0:T(8,128)(2,1)S(1)} %collective-permute-done.2.act_b, bf16[256,2560]{1,0:T(8,128)(2,1)S(1)} %convolution_convert_fusion.done_ref, ...), custom_call_target="tpu_custom_call" | custom-call | flops 1 | bytes 1 | tf_op jit(solution)/shard_map/grad_parts/pallas_call | solution.py:94
  125.5 2.5 %reshape.30 = bf16[128,2,5248]{2,1,0:T(2,128)(2,1)} reshape(bf16[256,5248]{1,0:T(8,128)(2,1)S(1)} %grad_parts.1) | data formatting | bytes 5373952 | tf_op jit(solution)/shard_map/reshape | solution.py:117
  128.0 74.2 %all_to_all.15 = bf16[128,2,5248]{2,1,0:T(2,128)(2,1)} all-to-all(bf16[128,2,5248]{2,1,0:T(2,128)(2,1)} %reshape.30), channel_id=1, replica_groups=mesh['section'=2,'tp'=4,'ep'=32] {'tp','ep'}, dimensions={0} | all-to-all | bytes 5373952 | tf_op jit(solution)/shard_map/all_to_all | solution.py:121
  202.2 5.4 %reshape.31 = bf16[256,5248]{1,0:T(8,128)(2,1)S(1)} reshape(bf16[128,2,5248]{2,1,0:T(2,128)(2,1)} %all_to_all.15) | data formatting | bytes 5373952 | tf_op jit(solution)/shard_map/reshape | solution.py:185
  (56 shorter events, 8.0 us)
Async XLA Ops:
  0.6 23.5 %copy-start = (bf16[32,2560]{1,0:T(8,128)(2,1)S(1)}, bf16[32,2560]{1,0:T(8,128)(2,1)}, u32[]{:S(2)}) copy-start(bf16[32,2560]{1,0:T(8,128)(2,1)} %param.15) | copy-start | bytes 491524
  1.8 3.7 %collective-permute-start = (f32[32,1]{1,0:T(8,128)S(1)}, f32[32,1]{1,0:T(8,128)S(1)}, u32[]{:S(2)}, u32[]{:S(2)}) collective-permute-start(f32[32,1]{1,0:T(8,128)S(1)} %copy.17), channel_id=1, source_target_pairs={{0,128},{128,0},{1,129},{129,1},{2,130},{130,2},{3,131},{131,3},{4... | collective-permute-start | bytes 392 | tf_op jit(solution)/shard_map/ppermute | solution.py:156
  8.6 51.5 %all-to-all-start = ((bf16[128,2,2560]{2,1,0:T(2,128)(2,1)}), bf16[128,2,2560]{2,1,0:T(2,128)(2,1)S(1)}, u32[]{:S(2)}, u32[]{:S(2)}) async-start(bf16[128,2,2560]{2,1,0:T(2,128)(2,1)} %reshape.26), calls=%async_computation | async-start | bytes 2621440 | tf_op jit(solution)/shard_map/all_to_all | solution.py:121
  60.1 43.8 %all-to-all-start.1 = ((bf16[128,2,2560]{2,1,0:T(2,128)(2,1)}), bf16[128,2,2560]{2,1,0:T(2,128)(2,1)}, u32[]{:S(2)}, u32[]{:S(2)}) async-start(bf16[128,2,2560]{2,1,0:T(2,128)(2,1)} %reshape.28), calls=%async_computation.1 | async-start | bytes 2621440 | tf_op jit(solution)/shard_map/all_to_all | solution.py:121
  68.7 3.5 %copy-start.3 = (bf16[1,2560,768]{2,1,0:T(8,128)(2,1)S(1)}, bf16[1,2560,768]{2,1,0:T(8,128)(2,1)}, u32[]{:S(2)}) copy-start(bf16[1,2560,768]{2,1,0:T(8,128)(2,1)} %param.12) | copy-start | bytes 11796484
  72.2 1.2 copy-start.9
  73.4 0.9 copy-start.11
  74.3 36.6 %copy-start.5 = (bf16[256,1536]{1,0:T(8,128)(2,1)}, bf16[256,1536]{1,0:T(8,128)(2,1)S(1)}, u32[]{:S(2)}) copy-start(bf16[256,1536]{1,0:T(8,128)(2,1)S(1)} %fusion.5.pre_a) | copy-start | bytes 2359300
  74.3 37.5 %collective-permute-start.1 = (bf16[256,1536]{1,0:T(8,128)(2,1)S(1)}, bf16[256,1536]{1,0:T(8,128)(2,1)S(1)}, u32[]{:S(2)}, u32[]{:S(2)}) collective-permute-start(bf16[256,1536]{1,0:T(8,128)(2,1)S(1)} %fusion.5.pre_a), channel_id=1, source_target_pairs={{0,128},{128,0},{1,129},{129,1},{2,130},{130,2},{3,131},{131,3},{4... | collective-permute-start | bytes 2359304 | tf_op jit(solution)/shard_map/ppermute | solution.py:175
  107.1 2.1 %copy-start.1 = (bf16[1,768,2560]{2,1,0:T(8,128)(2,1)S(1)}, bf16[1,768,2560]{2,1,0:T(8,128)(2,1)}, u32[]{:S(2)}) copy-start(bf16[1,768,2560]{2,1,0:T(8,128)(2,1)} %param.14) | copy-start | bytes 11796484
  109.2 2.6 %copy-start.10 = (f32[256,768]{1,0:T(8,128)S(1)}, f32[256,768]{1,0:T(8,128)}, u32[]{:S(2)}) copy-start(f32[256,768]{1,0:T(8,128)} %copy-done.9) | copy-start | bytes 2359300
  109.2 2.6 %copy-start.12 = (f32[256,768]{1,0:T(8,128)S(1)}, f32[256,768]{1,0:T(8,128)}, u32[]{:S(2)}) copy-start(f32[256,768]{1,0:T(8,128)} %copy-done.11) | copy-start | bytes 2359300
  110.9 9.4 %collective-permute-start.2 = (bf16[256,768]{1,0:T(8,128)(2,1)S(1)}, bf16[256,768]{1,0:T(8,128)(2,1)S(1)}, u32[]{:S(2)}, u32[]{:S(2)}) collective-permute-start(bf16[256,768]{1,0:T(8,128)(2,1)S(1)} %grad_act.1.act_a), channel_id=1, source_target_pairs={{0,128},{128,0},{1,129},{129,1},{2,130},{130,2},{3,131},{131,3},{4... | collective-permute-start | bytes 1179656 | tf_op jit(solution)/shard_map/ppermute | solution.py:183
  111.8 0.9 copy-start.7
  111.9 8.5 %copy-start.6 = (bf16[256,1536]{1,0:T(8,128)(2,1)S(1)}, bf16[256,1536]{1,0:T(8,128)(2,1)}, u32[]{:S(2)}) copy-start(bf16[256,1536]{1,0:T(8,128)(2,1)} %copy-done.5) | copy-start | bytes 2359300
  112.7 7.6 %copy-start.4 = (bf16[1,2560,768]{2,1,0:T(8,128)(2,1)S(1)}, bf16[1,2560,768]{2,1,0:T(8,128)(2,1)}, u32[]{:S(2)}) copy-start(bf16[1,2560,768]{2,1,0:T(8,128)(2,1)} %param.12) | copy-start | bytes 11796484
  113.0 7.4 %copy-start.2 = (bf16[1,2560,768]{2,1,0:T(8,128)(2,1)S(1)}, bf16[1,2560,768]{2,1,0:T(8,128)(2,1)}, u32[]{:S(2)}) copy-start(bf16[1,2560,768]{2,1,0:T(8,128)(2,1)} %param.13) | copy-start | bytes 11796484
  120.3 1.1 copy-start.8
  207.6 1.0 copy-start.15
  208.3 2.2 %copy-start.13 = (bf16[32,2560]{1,0:T(8,128)(2,1)S(1)}, bf16[32,2560]{1,0:T(8,128)(2,1)}, u32[]{:S(2)}) copy-start(bf16[32,2560]{1,0:T(8,128)(2,1)} %param.8) | copy-start | bytes 491524
  208.3 2.2 %copy-start.14 = (f32[2560]{0:T(1024)S(1)}, f32[2560]{0:T(1024)}, u32[]{:S(2)}) copy-start(f32[2560]{0:T(1024)} %param.9) | copy-start | bytes 30724

commit v3 on v2

--- a/solution.py
+++ b/solution.py
@@ -19,27 +19,67 @@
 
 
 SMALL = pl.CostEstimate(flops=1, bytes_accessed=1, transcendentals=0)
-ROOM = pltpu.CompilerParams(vmem_limit_bytes=40 * 1024 * 1024)
-
-
-def act_kernel(rows_ref, down_ref, out_ref):
-    out_ref[...] = contract_last(rows_ref[...], down_ref[...]).astype(BF)
+
+
+def room(mib):
+    return pltpu.CompilerParams(vmem_limit_bytes=mib * 1024 * 1024)
+
+
+def column_block(width):
+    return 512 if width % 512 == 0 else width
+
+
+def send_kernel(select_ref, tokens_ref, inv_ref, gain_ref, out_ref):
+    normed = (tokens_ref[...].astype(F32) * inv_ref[...] * gain_ref[...]).astype(BF)
+    rows = jnp.dot(select_ref[...], normed, preferred_element_type=F32).astype(BF)
+    out_ref[...] = rows.reshape(out_ref.shape)
+
+
+def token_messages(select, tokens, inv_rms, gain, peers):
+    tok_dev, half_dim = tokens.shape
+    slots = select.shape[0]
+    block = column_block(half_dim)
+    return pl.pallas_call(
+        send_kernel,
+        grid=(half_dim // block,),
+        in_specs=[
+            pl.BlockSpec((slots, tok_dev), lambda i: (0, 0)),
+            pl.BlockSpec((tok_dev, block), lambda i: (0, i)),
+            pl.BlockSpec((tok_dev, 1), lambda i: (0, 0)),
+            pl.BlockSpec((1, block), lambda i: (0, i)),
+        ],
+        out_specs=pl.BlockSpec((peers, slots // peers, block), lambda i: (0, 0, i)),
+        out_shape=jax.ShapeDtypeStruct((peers, slots // peers, half_dim), BF),
+        compiler_params=room(16),
+        cost_estimate=SMALL,
+        name="token_messages",
+    )(select, tokens, inv_rms, gain.reshape(1, half_dim))
+
+
+def act_kernel(rows_ref, down_ref, out_ref, kept):
+    @pl.when(pl.program_id(0) == 0)
+    def _():
+        kept[...] = rows_ref[...].reshape(kept.shape)
+
+    out_ref[...] = contract_last(kept[...], down_ref[...]).astype(BF)
 
 
 def grad_act_part(rows, down_mat):
-    slots, half_dim = rows.shape
+    peers, per_peer, half_dim = rows.shape
+    slots = peers * per_peer
     ff_dim = down_mat.shape[0]
-    block = 256
+    block = ff_dim // 3
     return pl.pallas_call(
         act_kernel,
-        grid=(ff_dim // block,),
+        grid=(3,),
         in_specs=[
-            pl.BlockSpec((slots, half_dim), lambda i: (0, 0)),
+            pl.BlockSpec((peers, per_peer, half_dim), lambda i: (0, 0, 0)),
             pl.BlockSpec((block, half_dim), lambda i: (i, 0)),
         ],
         out_specs=pl.BlockSpec((slots, block), lambda i: (0, i)),
         out_shape=jax.ShapeDtypeStruct((slots, ff_dim), BF),
-        compiler_params=ROOM,
+        scratch_shapes=[pltpu.VMEM((slots, half_dim), BF)],
+        compiler_params=room(24),
         cost_estimate=SMALL,
         name="grad_act",
     )(rows, down_mat)
@@ -52,11 +92,12 @@
 
 
 def part_kernel(
-    pre_a, pre_b, act_a, act_b, done_ref, gate_ref, up_ref, out_ref, gate_grad, up_grad
+    top_k, pre_a, pre_b, act_a, act_b, done_ref, gate_ref, up_ref, out_ref, gate_grad, up_grad
 ):
     ff_dim = act_a.shape[1]
     half_dim = done_ref.shape[1]
     block = gate_ref.shape[0]
+    peers, per_peer, _ = out_ref.shape
     step = pl.program_id(0)
 
     @pl.when(step == 0)
@@ -75,42 +116,122 @@
         lane = lax.broadcasted_iota(jnp.int32, (done_ref.shape[0], 128), 1)
         sums = jnp.zeros(lane.shape, F32)
         for at, part in enumerate(in_pieces(weight_dot) + in_pieces(mean_dot)):
-            sums = jnp.where(lane == at, part, sums)
-        out_ref[:, 2 * half_dim :] = sums.astype(BF)
-        out_ref[:, :half_dim] = done_ref[...]
+            sums = jnp.where((lane >= at * top_k) & (lane < (at + 1) * top_k), part, sums)
+        out_ref[:, :, 2 * half_dim :] = sums.astype(BF).reshape(peers, per_peer, 128)
+        out_ref[:, :, :half_dim] = done_ref[...].reshape(peers, per_peer, half_dim)
 
     columns = pl.ds(pl.multiple_of(half_dim + step * block, 128), block)
-    out_ref[:, columns] = (
-        contract_last(gate_grad[...], gate_ref[...]) + contract_last(up_grad[...], up_ref[...])
-    ).astype(BF)
-
-
-def grad_parts(own_pre, other_pre, own_act, other_act, expert_out, gate_mat, up_mat):
+    part = contract_last(gate_grad[...], gate_ref[...]) + contract_last(up_grad[...], up_ref[...])
+    out_ref[:, :, columns] = part.astype(BF).reshape(peers, per_peer, block)
+
+
+def grad_parts(own_pre, other_pre, own_act, other_act, expert_out, gate_mat, up_mat, peers, top_k):
     slots, ff_dim = own_act.shape
     half_dim = gate_mat.shape[0]
-    block = 512
+    block = column_block(half_dim)
+    shape = (peers, slots // peers, 2 * half_dim + 128)
     whole = lambda width: pl.BlockSpec((slots, width), lambda i: (0, 0))
     weights = pl.BlockSpec((block, ff_dim), lambda i: (i, 0))
+
+    def body(*refs):
+        part_kernel(top_k, *refs)
+
     return pl.pallas_call(
-        part_kernel,
+        body,
         grid=(half_dim // block,),
         in_specs=[whole(2 * ff_dim)] * 2 + [whole(ff_dim)] * 2 + [whole(half_dim)] + [weights] * 2,
-        out_specs=whole(2 * half_dim + 128),
-        out_shape=jax.ShapeDtypeStruct((slots, 2 * half_dim + 128), BF),
+        out_specs=pl.BlockSpec(shape, lambda i: (0, 0, 0)),
+        out_shape=jax.ShapeDtypeStruct(shape, BF),
         scratch_shapes=[pltpu.VMEM((slots, ff_dim), BF)] * 2,
-        compiler_params=ROOM,
+        compiler_params=room(40),
         cost_estimate=SMALL,
         name="grad_parts",
     )(own_pre, other_pre, own_act, other_act, expert_out, gate_mat, up_mat)
 
 
+def finish_kernel(
+    top_k,
+    full_dim,
+    out_rows,
+    grad_rows,
+    sum_rows,
+    weights_ref,
+    select_ref,
+    slot_k_ref,
+    inv_ref,
+    tokens_ref,
+    gain_ref,
+    routed_ref,
+    grad_ref,
+    slot_ref,
+    mean_ref,
+):
+    tok_dev = inv_ref.shape[0]
+    slots = select_ref.shape[1]
+
+    @pl.when(pl.program_id(0) == 0)
+    def _():
+        lane = lax.broadcasted_iota(jnp.int32, (slots, 128), 1)
+        sums = sum_rows[...].reshape(slots, 128).astype(F32)
+        sums = jnp.where((lane % top_k).astype(F32) == slot_k_ref[...], sums, 0.0).astype(BF)
+        tail = jnp.dot(select_ref[...], sums, preferred_element_type=F32)
+        slot_ref[...] = tail
+        at = lax.broadcasted_iota(jnp.int32, tail.shape, 1)
+        mean = jnp.where((at >= 3 * top_k) & (at < 6 * top_k), tail, 0.0)
+        mean = jnp.sum(mean, axis=1, keepdims=True) / inv_ref[...] / full_dim
+        mean_ref[...] = jnp.broadcast_to(mean, mean_ref.shape)
+
+    outs = out_rows[...].reshape(slots, routed_ref.shape[1])
+    halves = jnp.dot(weights_ref[...], outs, preferred_element_type=F32)
+    routed_ref[...] = (halves[:tok_dev] + halves[tok_dev:]).astype(BF)
+    grads = grad_rows[...].reshape(slots, routed_ref.shape[1])
+    scaled = jnp.dot(select_ref[...], grads, preferred_element_type=F32) * gain_ref[...]
+    inv = inv_ref[...]
+    drop = tokens_ref[...].astype(F32) * (inv * inv * inv) * mean_ref[:, :1]
+    grad_ref[...] = (inv * scaled - drop).astype(BF)
+
+
+def finish(back, weights_t, select_t, slot_k, inv_rms, tokens, gain, top_k, full_dim):
+    peers, per_peer, _ = back.shape
+    tok_dev, half_dim = tokens.shape
+    slots = peers * per_peer
+    block = column_block(half_dim)
+    steps = half_dim // block
+    fixed = lambda shape: pl.BlockSpec(shape, lambda i: (0, 0))
+    moving = lambda rows: pl.BlockSpec((rows, block), lambda i: (0, i))
+
+    def body(*refs):
+        finish_kernel(top_k, full_dim, *refs)
+
+    return pl.pallas_call(
+        body,
+        grid=(steps,),
+        in_specs=[
+            pl.BlockSpec((peers, per_peer, block), lambda i: (0, 0, i)),
+            pl.BlockSpec((peers, per_peer, block), lambda i: (0, 0, steps + i)),
+            pl.BlockSpec((peers, per_peer, 128), lambda i: (0, 0, 2 * half_dim // 128)),
+            fixed((2 * tok_dev, slots)),
+            fixed((tok_dev, slots)),
+            fixed((slots, 1)),
+            fixed((tok_dev, 1)),
+            moving(tok_dev),
+            moving(1),
+        ],
+        out_specs=[moving(tok_dev), moving(tok_dev), fixed((tok_dev, 128))],
+        out_shape=[
+            jax.ShapeDtypeStruct((tok_dev, half_dim), BF),
+            jax.ShapeDtypeStruct((tok_dev, half_dim), BF),
+            jax.ShapeDtypeStruct((tok_dev, 128), F32),
+        ],
+        scratch_shapes=[pltpu.VMEM((tok_dev, 128), F32)],
+        compiler_params=room(16),
+        cost_estimate=SMALL,
+        name="finish",
+    )(back, back, back, weights_t, select_t, slot_k, inv_rms, tokens, gain.reshape(1, half_dim))
+
+
 def rounded(value):
     return lax.reduce_precision(value, exponent_bits=8, mantissa_bits=7)
-
-
-def unpacked(block, at):
-    block = block.astype(F32)
-    return block[:, 3 * at : 3 * at + 1] + block[:, 3 * at + 1 : 3 * at + 2] + block[:, 3 * at + 2 : 3 * at + 3]
 
 
 def blocks(rows, devices):
@@ -154,9 +275,7 @@
     tokens_f = tokens.astype(F32)
     squares = jnp.sum(tokens_f * tokens_f, axis=1, keepdims=True)
     inv_rms = lax.rsqrt((squares + lax.ppermute(squares, "section", swap)) / full_dim + EPS)
-    normed = (tokens_f * inv_rms * gain).astype(BF)
-    outgoing = jnp.dot(select, normed, preferred_element_type=F32).astype(BF)
-    arrived = exchange(blocks(outgoing, experts)).reshape(slots, half_dim)
+    arrived = exchange(token_messages(select, tokens, inv_rms, gain, experts)).reshape(slots, half_dim)
     grad_rows = (
         slot_weight * jnp.dot(select, grad_out, preferred_element_type=F32)
     ).astype(BF)
@@ -178,35 +297,26 @@
     sigmoid_gate = jax.nn.sigmoid(pre_gate)
     activated = lax.optimization_barrier((pre_gate * sigmoid_gate * pre_up).astype(BF))
     expert_out = jnp.dot(activated, down_mat, preferred_element_type=F32).astype(BF)
-    grad_arrived = grad_blocks.reshape(slots, half_dim)
-    own_act = grad_act_part(grad_arrived, down_mat)
+    own_act = grad_act_part(grad_blocks, down_mat)
     other_act = lax.ppermute(own_act, "section", swap)
-    parts = grad_parts(pre_send, other_pre, own_act, other_act, expert_out, gate_mat, up_mat)
-    back = exchange(blocks(parts, experts)).reshape(parts.shape)
-    returned, back = back[:, :half_dim], back[:, half_dim:]
+    parts = grad_parts(
+        pre_send, other_pre, own_act, other_act, expert_out, gate_mat, up_mat, experts, top_k
+    )
+    back = exchange(parts)
 
     weight_high = rounded(weighted)
     weight_low = weighted - weight_high
-    halves = contract_first(
-        jnp.concatenate([weight_high, weight_low], axis=1).astype(BF), returned
-    )
-    routed = (halves[:tok_dev] + halves[tok_dev:]).astype(BF)
-
-    summed = contract_first(select, back)
-    mean_total = unpacked(summed[:, half_dim:], 1) / inv_rms
-    slot_dot = unpacked(back[:, half_dim:], 0)
-    grad_weights = (
-        jnp.stack(
-            [
-                jnp.sum(jnp.where(named[k] & at_rank, slot_dot, 0.0), axis=0)
-                for k in range(top_k)
-            ],
-            axis=1,
-        )
-        / route_weights
-    )
-    scaled = summed[:, :half_dim] * gain
-    grad_tokens = (inv_rms * scaled - tokens_f * inv_rms**3 * (mean_total / full_dim)).astype(BF)
+    slot_k = jnp.sum(
+        sum(jnp.where(n & at_rank, float(k), 0.0) for k, n in enumerate(named)),
+        axis=1,
+        keepdims=True,
+    )
+    weights_both = jnp.concatenate([weight_high, weight_low], axis=1).astype(BF).T
+    routed, grad_tokens, tail = finish(
+        back, weights_both, select.T, slot_k, inv_rms, tokens, gain, top_k, full_dim
+    )
+    slot_dot = tail[:, :top_k] + tail[:, top_k : 2 * top_k] + tail[:, 2 * top_k : 3 * top_k]
+    grad_weights = slot_dot / route_weights
     return (routed, grad_tokens, grad_weights)
 
 

time: 212 us -> 204 us (0.962)
  blocking collectives: 74.2 us -> 0 us
  waiting for transfers between devices: 69 us -> 134 us
  local copies, waits for them, and re-layouts: 21 us -> 12 us
  starting transfers between devices: 26.8 us -> 34.2 us
  Pallas kernels: 5.67 us -> 12.5 us
  other arithmetic: 4.56 us -> 1.98 us
    all_to_all x1 -> x0, blocking collectives: 74.2 us -> none  [exchange(): lax.all_to_all(blocked, ('tp', 'ep'), split_axis=0, concat_axis=0, tiled=...]
    all_to_all x2 -> x3, waiting for transfers between devices: 62.9 us -> 127 us  [exchange(): lax.all_to_all(blocked, ('tp', 'ep'), split_axis=0, concat_axis=0, tiled=...]
    all_to_all x2 -> x3, starting transfers between devices: 23.6 us -> 32 us  [exchange(): lax.all_to_all(blocked, ('tp', 'ep'), split_axis=0, concat_axis=0, tiled=...]
    reshape x3 -> x2, local copies, waits for them, and re-layouts: 9.13 us -> 2.07 us  [the longest x1 1.35 us: local(): exchange(token_messages(select, tokens, inv_rms, gain, experts))]
    pallas_call x2 -> x4, Pallas kernels: 5.67 us -> 12.5 us  [the longest x1 4.27 us: grad_parts(): pl.pallas_call(body, grid=(half_dim // block,), in_specs=[whole(2 * ff_di...]
    reshape x3 -> x1, local copies, waits for them, and re-layouts: 5.25 us -> 1.38 us  [blocks(): return rows.reshape(devices, rows.shape[0] // devices, rows.shape[1])]
    dot_general x3 -> x0, matrix products: 2.29 us -> none  [the longest x1 1.54 us: local(): outgoing = jnp.dot(select, normed, preferred_element_type=F32).astype(BF)]
    unnamed x32 -> x30, local copies, waits for them, and re-layouts: 4.72 us -> 6.34 us
  transfers between devices with their start and end apart: 5 -> 6, of which waited for: 3 -> 4; matrix products, arithmetic and copies ran while one was open for 7% -> 7% of each run, Pallas kernels for 1% -> 1%
where the time goes in v3:
time: 204 us; the launch traced here: 203 us
  waiting for transfers between devices  134 us (66%)
  starting transfers between devices  34.2 us (17%)
  Pallas kernels  12.5 us (6%)
  local copies, waits for them, and re-layouts  12 us (6%)
  matrix products  7.07 us (3%)
    all_to_all x3, waiting for transfers between devices, exchange(): lax.all_to_all(blocked, ('tp', 'ep'), split_axis=0, concat_axis=0, tiled=...  127 us
    all_to_all x3, starting transfers between devices, exchange(): lax.all_to_all(blocked, ('tp', 'ep'), split_axis=0, concat_axis=0, tiled=...  32 us
    ppermute x1, waiting for transfers between devices, local(): other_act = lax.ppermute(own_act, 'section', swap)  7.31 us
    unnamed x30, local copies, waits for them, and re-layouts  6.34 us
    pallas_call x1, Pallas kernels, grad_parts(): pl.pallas_call(body, grid=(half_dim // block,), in_specs=[whole(2 * ff_di...  4.27 us
  transfers between devices with their start and end apart: 6, of which 4 were waited for; matrix products, arithmetic and copies ran while one was open for 7% of the time, Pallas kernels for 1%

profile of v3, /device:TPU:2, one launch (start us, length us, event | category | flops | bytes accessed | tf_op | source)
XLA Modules:
  0.0 203.0 jit_solution(16652063227408887773)
XLA Ops:
  0.6 1.1 multiply_reduce_fusion
  1.7 1.7 collective-permute-start
  3.4 0.9 slice_bitcast_fusion.11
  4.3 0.9 slice_bitcast_fusion.5
  6.6 0.9 copy-done.6
  7.5 3.0 %token_messages.1 = bf16[128,2,2560]{2,1,0:T(2,128)(2,1)} custom-call(bf16[256,32]{1,0:T(8,128)(2,1)S(1)} %copy.23.select_ref, bf16[32,2560]{1,0:T(8,128)(2,1)S(1)} %copy-done.6, f32[32,1]{1,0:T(8,128)S(1)} %add_rsqrt_fusion.inv_ref.refs_6_, f32[1,2560]{1,0:T(1,128)S(1)} %reshape.17.gain_ref.refs_8_), custom_call_target="tpu_custom_call" | custom-call | flops 1 | bytes 1 | tf_op jit(solution)/shard_map/token_messages/pallas_call | solution.py:42
  10.5 15.2 %all-to-all-start = ((bf16[128,2,2560]{2,1,0:T(2,128)(2,1)}), bf16[128,2,2560]{2,1,0:T(2,128)(2,1)S(1)}, u32[]{:S(2)}, u32[]{:S(2)}) async-start(bf16[128,2,2560]{2,1,0:T(2,128)(2,1)} %token_messages.1), calls=%async_computation | async-start | bytes 2621440 | tf_op jit(solution)/shard_map/all_to_all | solution.py:242
  26.4 1.4 reshape.19
  27.8 33.9 %all-to-all-done = bf16[128,2,2560]{2,1,0:T(2,128)(2,1)S(1)} async-done(((bf16[128,2,2560]{2,1,0:T(2,128)(2,1)}), bf16[128,2,2560]{2,1,0:T(2,128)(2,1)S(1)}, u32[]{:S(2)}, u32[]{:S(2)}) %all-to-all-start) | async-done | bytes 1310752 | tf_op jit(solution)/shard_map/all_to_all | solution.py:242
  61.7 7.7 %all-to-all-start.1 = ((bf16[128,2,2560]{2,1,0:T(2,128)(2,1)}), bf16[128,2,2560]{2,1,0:T(2,128)(2,1)S(1)}, u32[]{:S(2)}, u32[]{:S(2)}) async-start(bf16[128,2,2560]{2,1,0:T(2,128)(2,1)} %reshape.19), calls=%async_computation.1 | async-start | bytes 2621440 | tf_op jit(solution)/shard_map/all_to_all | solution.py:242
  69.4 1.4 reshape.18
  70.7 3.8 %fusion.27 = f32[256,768]{1,0:T(8,128)S(1)} fusion(bf16[256,2560]{1,0:T(8,128)(2,1)} %reshape.18, bf16[1,2560,768]{2,1,0:T(8,128)(2,1)} %param.13), kind=kOutput, calls=%fused_computation.74 | convolution fusion | flops 1006632960 | bytes 6029312 | tf_op jit(solution)/shard_map/dot_general | solution.py:288
  74.8 1.2 fusion.29
  76.1 0.8 copy-done.10
  77.0 28.4 %all-to-all-done.1.rows_ref = bf16[128,2,2560]{2,1,0:T(2,128)(2,1)S(1)} async-done(((bf16[128,2,2560]{2,1,0:T(2,128)(2,1)}), bf16[128,2,2560]{2,1,0:T(2,128)(2,1)S(1)}, u32[]{:S(2)}, u32[]{:S(2)}) %all-to-all-start.1) | async-done | bytes 1310752 | tf_op jit(solution)/shard_map/all_to_all | solution.py:242
  105.4 2.1 %copy-done.2 = bf16[1,768,2560]{2,1,0:T(8,128)(2,1)S(1)} copy-done((bf16[1,768,2560]{2,1,0:T(8,128)(2,1)S(1)}, bf16[1,768,2560]{2,1,0:T(8,128)(2,1)}, u32[]{:S(2)}) %copy-start.2) | copy-done | bytes 3932184
  107.5 1.8 grad_act.1.refs_2_
  110.2 1.2 convolution_convert_fusion.refs_4_
  111.4 7.3 %collective-permute-done.2.refs_3_ = bf16[256,768]{1,0:T(8,128)(2,1)S(1)} collective-permute-done((bf16[256,768]{1,0:T(8,128)(2,1)S(1)}, bf16[256,768]{1,0:T(8,128)(2,1)S(1)}, u32[]{:S(2)}, u32[]{:S(2)}) %collective-permute-start.2) | collective-permute-done | bytes 393248 | tf_op jit(solution)/shard_map/ppermute | solution.py:301
  118.8 4.3 %grad_parts.1 = bf16[128,2,5248]{2,1,0:T(2,128)(2,1)S(1)} custom-call(bf16[256,1536]{1,0:T(8,128)(2,1)S(1)} %fusion.1.refs_0_, bf16[256,1536]{1,0:T(8,128)(2,1)S(1)} %collective-permute-done.1.refs_1_, bf16[256,768]{1,0:T(8,128)(2,1)S(1)} %grad_act.1.refs_2_, bf16[256,768]{1,0:T(8,128)(2,1)S(1)} %collective-permute-done.2.refs_3_, ...), custom_call_target="tpu_custom_call" | custom-call | flops 1 | bytes 1 | tf_op jit(solution)/shard_map/grad_parts/pallas_call | solution.py:139
  123.0 1.5 copy-done.1
  124.6 9.1 %all-to-all-start.2 = ((bf16[128,2,5248]{2,1,0:T(2,128)(2,1)}), bf16[128,2,5248]{2,1,0:T(2,128)(2,1)S(1)}, u32[]{:S(2)}, u32[]{:S(2)}) async-start(bf16[128,2,5248]{2,1,0:T(2,128)(2,1)} %copy-done.1), calls=%async_computation.2 | async-start | bytes 5373952 | tf_op jit(solution)/shard_map/all_to_all | solution.py:242
  134.0 64.8 %all-to-all-done.2.refs_0_.refs_1_.refs_2_ = bf16[128,2,5248]{2,1,0:T(2,128)(2,1)S(1)} async-done(((bf16[128,2,5248]{2,1,0:T(2,128)(2,1)}), bf16[128,2,5248]{2,1,0:T(2,128)(2,1)S(1)}, u32[]{:S(2)}, u32[]{:S(2)}) %all-to-all-start.2) | async-done | bytes 2687008 | tf_op jit(solution)/shard_map/all_to_all | solution.py:242
  198.8 3.4 %finish.1 = (bf16[32,2560]{1,0:T(8,128)(2,1)}, bf16[32,2560]{1,0:T(8,128)(2,1)}, f32[32,128]{1,0:T(8,128)S(1)}) custom-call(bf16[128,2,5248]{2,1,0:T(2,128)(2,1)S(1)} %all-to-all-done.2.refs_0_.refs_1_.refs_2_, bf16[128,2,5248]{2,1,0:T(2,128)(2,1)S(1)} %all-to-all-done.2.refs_0_.refs_1_.refs_2_, ...), custom_call_target="tpu_custom_call" | custom-call | flops 1 | bytes 1 | tf_op jit(solution)/shard_map/finish/pallas_call | solution.py:206
  (49 shorter events, 4.4 us)
Async XLA Ops:
  0.6 25.1 %copy-start = (bf16[32,2560]{1,0:T(8,128)(2,1)S(1)}, bf16[32,2560]{1,0:T(8,128)(2,1)}, u32[]{:S(2)}) copy-start(bf16[32,2560]{1,0:T(8,128)(2,1)} %param.15) | copy-start | bytes 491524
  1.7 4.7 %collective-permute-start = (f32[32,1]{0,1:T(1,128)S(1)}, f32[32,1]{0,1:T(1,128)S(1)}, u32[]{:S(2)}, u32[]{:S(2)}) collective-permute-start(f32[32,1]{0,1:T(1,128)S(1)} %bitcast.54), channel_id=1, source_target_pairs={{0,128},{128,0},{1,129},{129,1},{2,130},{130,2},{3,131},{131,3},{4... | collective-permute-start | bytes 392 | tf_op jit(solution)/shard_map/ppermute | solution.py:277
  6.6 0.9 copy-start.6
  10.5 51.2 %all-to-all-start = ((bf16[128,2,2560]{2,1,0:T(2,128)(2,1)}), bf16[128,2,2560]{2,1,0:T(2,128)(2,1)S(1)}, u32[]{:S(2)}, u32[]{:S(2)}) async-start(bf16[128,2,2560]{2,1,0:T(2,128)(2,1)} %token_messages.1), calls=%async_computation | async-start | bytes 2621440 | tf_op jit(solution)/shard_map/all_to_all | solution.py:242
  61.7 43.7 %all-to-all-start.1 = ((bf16[128,2,2560]{2,1,0:T(2,128)(2,1)}), bf16[128,2,2560]{2,1,0:T(2,128)(2,1)S(1)}, u32[]{:S(2)}, u32[]{:S(2)}) async-start(bf16[128,2,2560]{2,1,0:T(2,128)(2,1)} %reshape.19), calls=%async_computation.1 | async-start | bytes 2621440 | tf_op jit(solution)/shard_map/all_to_all | solution.py:242
  70.7 3.8 %copy-start.4 = (bf16[1,2560,768]{2,1,0:T(8,128)(2,1)S(1)}, bf16[1,2560,768]{2,1,0:T(8,128)(2,1)}, u32[]{:S(2)}) copy-start(bf16[1,2560,768]{2,1,0:T(8,128)(2,1)} %param.12) | copy-start | bytes 11796484
  70.7 4.1 %copy-start.12 = (bf16[256,2560]{1,0:T(8,128)(2,1)S(1)}, bf16[256,2560]{1,0:T(8,128)(2,1)}, u32[]{:S(2)}) copy-start(bf16[256,2560]{1,0:T(8,128)(2,1)} %reshape.18) | copy-start | bytes 3932164
  74.8 1.2 copy-start.8
  76.0 0.9 copy-start.10
  76.9 32.9 %collective-permute-start.1 = (bf16[256,1536]{1,0:T(8,128)(2,1)S(1)}, bf16[256,1536]{1,0:T(8,128)(2,1)S(1)}, u32[]{:S(2)}, u32[]{:S(2)}) collective-permute-start(bf16[256,1536]{1,0:T(8,128)(2,1)S(1)} %fusion.1.refs_0_), channel_id=1, source_target_pairs={{0,128},{128,0},{1,129},{129,1},{2,130},{130,2},{3,131},{131,3},{4... | collective-permute-start | bytes 2359304 | tf_op jit(solution)/shard_map/ppermute | solution.py:294
  105.4 2.1 %copy-start.2 = (bf16[1,768,2560]{2,1,0:T(8,128)(2,1)S(1)}, bf16[1,768,2560]{2,1,0:T(8,128)(2,1)}, u32[]{:S(2)}) copy-start(bf16[1,768,2560]{2,1,0:T(8,128)(2,1)} %param.14) | copy-start | bytes 11796484
  107.5 2.2 %copy-start.9 = (f32[256,768]{1,0:T(8,128)S(1)}, f32[256,768]{1,0:T(8,128)}, u32[]{:S(2)}) copy-start(f32[256,768]{1,0:T(8,128)} %copy-done.8) | copy-start | bytes 2359300
  107.5 2.2 %copy-start.11 = (f32[256,768]{1,0:T(8,128)S(1)}, f32[256,768]{1,0:T(8,128)}, u32[]{:S(2)}) copy-start(f32[256,768]{1,0:T(8,128)} %copy-done.10) | copy-start | bytes 2359300
  109.3 9.4 %collective-permute-start.2 = (bf16[256,768]{1,0:T(8,128)(2,1)S(1)}, bf16[256,768]{1,0:T(8,128)(2,1)S(1)}, u32[]{:S(2)}, u32[]{:S(2)}) collective-permute-start(bf16[256,768]{1,0:T(8,128)(2,1)S(1)} %grad_act.1.refs_2_), channel_id=1, source_target_pairs={{0,128},{128,0},{1,129},{129,1},{2,130},{130,2},{3,131},{131,3},{4... | collective-permute-start | bytes 1179656 | tf_op jit(solution)/shard_map/ppermute | solution.py:301
  110.0 8.8 %copy-start.5 = (bf16[1,2560,768]{2,1,0:T(8,128)(2,1)S(1)}, bf16[1,2560,768]{2,1,0:T(8,128)(2,1)}, u32[]{:S(2)}) copy-start(bf16[1,2560,768]{2,1,0:T(8,128)(2,1)} %param.12) | copy-start | bytes 11796484
  110.2 8.5 %copy-start.3 = (bf16[1,2560,768]{2,1,0:T(8,128)(2,1)S(1)}, bf16[1,2560,768]{2,1,0:T(8,128)(2,1)}, u32[]{:S(2)}) copy-start(bf16[1,2560,768]{2,1,0:T(8,128)(2,1)} %param.13) | copy-start | bytes 11796484
  123.0 1.5 copy-start.1
  124.6 9.1 %copy-start.13 = (f32[32,6]{0,1:T(8,128)S(1)}, f32[32,6]{0,1:T(8,128)}, u32[]{:S(2)}) copy-start(f32[32,6]{0,1:T(8,128)} %param.11) | copy-start | bytes 2308
  124.6 74.3 %copy-start.7 = (bf16[32,2560]{1,0:T(8,128)(2,1)S(1)}, bf16[32,2560]{1,0:T(8,128)(2,1)}, u32[]{:S(2)}) copy-start(bf16[32,2560]{1,0:T(8,128)(2,1)} %refs_7_.1) | copy-start | bytes 491524
  124.6 74.3 %all-to-all-start.2 = ((bf16[128,2,5248]{2,1,0:T(2,128)(2,1)}), bf16[128,2,5248]{2,1,0:T(2,128)(2,1)S(1)}, u32[]{:S(2)}, u32[]{:S(2)}) async-start(bf16[128,2,5248]{2,1,0:T(2,128)(2,1)} %copy-done.1), calls=%async_computation.2 | async-start | bytes 5373952 | tf_op jit(solution)/shard_map/all_to_all | solution.py:242

commit v4 on v3

--- a/solution.py
+++ b/solution.py
@@ -3,11 +3,12 @@
 from jax import lax
 from jax.experimental import pallas as pl
 from jax.experimental.pallas import tpu as pltpu
-from jax.sharding import PartitionSpec as P
+from jax.sharding import Mesh, PartitionSpec as P
 
 EPS = 1e-06
 BF = jnp.bfloat16
 F32 = jnp.float32
+CORES = 2
 
 
 def contract_last(left, right):
@@ -29,31 +30,38 @@
     return 512 if width % 512 == 0 else width
 
 
-def send_kernel(select_ref, tokens_ref, inv_ref, gain_ref, out_ref):
-    normed = (tokens_ref[...].astype(F32) * inv_ref[...] * gain_ref[...]).astype(BF)
-    rows = jnp.dot(select_ref[...], normed, preferred_element_type=F32).astype(BF)
-    out_ref[...] = rows.reshape(out_ref.shape)
-
-
-def token_messages(select, tokens, inv_rms, gain, peers):
+def send_kernel(select_ref, own_ref, mate_ref, own_inv, mate_inv, gain_ref, out_ref):
+    tok_dev = own_ref.shape[0]
+    own = (own_ref[...].astype(F32) * own_inv[...] * gain_ref[...]).astype(BF)
+    mate = (mate_ref[...].astype(F32) * mate_inv[...] * gain_ref[...]).astype(BF)
+    rows = jnp.dot(select_ref[:, :tok_dev], own, preferred_element_type=F32)
+    rows += jnp.dot(select_ref[:, tok_dev:], mate, preferred_element_type=F32)
+    out_ref[...] = rows.astype(BF).reshape(out_ref.shape)
+
+
+def token_messages(select, tokens, mate_tokens, inv_rms, mate_inv, gain, chips):
     tok_dev, half_dim = tokens.shape
     slots = select.shape[0]
-    block = column_block(half_dim)
+    block = half_dim // 2
+    moving = lambda rows: pl.BlockSpec((rows, block), lambda i: (0, i))
+    column = pl.BlockSpec((tok_dev, 1), lambda i: (0, 0))
     return pl.pallas_call(
         send_kernel,
         grid=(half_dim // block,),
         in_specs=[
-            pl.BlockSpec((slots, tok_dev), lambda i: (0, 0)),
-            pl.BlockSpec((tok_dev, block), lambda i: (0, i)),
-            pl.BlockSpec((tok_dev, 1), lambda i: (0, 0)),
-            pl.BlockSpec((1, block), lambda i: (0, i)),
+            pl.BlockSpec((slots, CORES * tok_dev), lambda i: (0, 0)),
+            moving(tok_dev),
+            moving(tok_dev),
+            column,
+            column,
+            moving(1),
         ],
-        out_specs=pl.BlockSpec((peers, slots // peers, block), lambda i: (0, 0, i)),
-        out_shape=jax.ShapeDtypeStruct((peers, slots // peers, half_dim), BF),
+        out_specs=pl.BlockSpec((chips, slots // chips, block), lambda i: (0, 0, i)),
+        out_shape=jax.ShapeDtypeStruct((chips, slots // chips, half_dim), BF),
         compiler_params=room(16),
         cost_estimate=SMALL,
         name="token_messages",
-    )(select, tokens, inv_rms, gain.reshape(1, half_dim))
+    )(select, tokens, mate_tokens, inv_rms, mate_inv, gain.reshape(1, half_dim))
 
 
 def act_kernel(rows_ref, down_ref, out_ref, kept):
@@ -238,8 +246,8 @@
     return rows.reshape(devices, rows.shape[0] // devices, rows.shape[1])
 
 
-def exchange(blocked):
-    return lax.all_to_all(blocked, ("tp", "ep"), split_axis=0, concat_axis=0, tiled=True)
+def exchange(blocked, axes):
+    return lax.all_to_all(blocked, axes, split_axis=0, concat_axis=0, tiled=True)
 
 
 def local(tokens, gain, routes, route_weights, w_gate, w_up, w_down, grad_out):
@@ -247,7 +255,7 @@
     top_k = routes.shape[1]
     section_size = lax.axis_size("section")
     full_dim = half_dim * section_size
-    experts = lax.axis_size("tp") * lax.axis_size("ep")
+    experts = lax.axis_size("tp") * lax.axis_size("zy") * CORES
     cap_src = max(2, tok_dev * top_k // experts + 1)
     slots = experts * cap_src
     gate_mat, up_mat, down_mat = (w_gate[0], w_up[0], w_down[0])
@@ -270,16 +278,53 @@
     weighted = sum(
         jnp.where(named[k] & at_rank, weights_t[k : k + 1, :], 0.0) for k in range(top_k)
     )
-    slot_weight = jnp.sum(weighted, axis=1, keepdims=True)
-
+
+    flip = [(0, 1), (1, 0)]
+    core = lax.axis_index("core")
+    chips = experts // CORES
+    pair = CORES * tok_dev
     tokens_f = tokens.astype(F32)
     squares = jnp.sum(tokens_f * tokens_f, axis=1, keepdims=True)
-    inv_rms = lax.rsqrt((squares + lax.ppermute(squares, "section", swap)) / full_dim + EPS)
-    arrived = exchange(token_messages(select, tokens, inv_rms, gain, experts)).reshape(slots, half_dim)
+    other_squares = lax.ppermute(squares, "section", swap)
+    mate_tokens = lax.ppermute(tokens, "core", flip)
+    mate_other = lax.ppermute(squares, ("section", "core"), [(i, 3 - i) for i in range(4)])
+    facts = jnp.concatenate([routes.astype(F32), route_weights], axis=1)
+    mate_facts = lax.ppermute(facts, "core", flip)
+    mate_grad = lax.ppermute(grad_out, "core", flip)
+    mate_f = mate_tokens.astype(F32)
+    mate_squares = jnp.sum(mate_f * mate_f, axis=1, keepdims=True)
+    inv_rms = lax.rsqrt((squares + other_squares) / full_dim + EPS)
+    mate_inv = lax.rsqrt((mate_squares + mate_other) / full_dim + EPS)
+
+    facts_t = jnp.concatenate([facts, mate_facts], axis=0).T
+    row = lax.broadcasted_iota(jnp.int32, (slots, pair), 0)
+    column = lax.broadcasted_iota(jnp.int32, (slots, pair), 1)
+    wanted = (row // (CORES * cap_src) * CORES + core).astype(F32)
+    here = row // cap_src % CORES == (column // tok_dev + core) % CORES
+    pair_named = [(facts_t[k : k + 1, :] == wanted) & here for k in range(top_k)]
+    pair_member = sum(n.astype(F32) for n in pair_named)
+    before = lax.broadcasted_iota(jnp.int32, (pair, pair), 0)
+    after = lax.broadcasted_iota(jnp.int32, (pair, pair), 1)
+    pair_earlier = (before // tok_dev == after // tok_dev) & (before < after)
+    pair_rank = jnp.dot(
+        pair_member.astype(BF), pair_earlier.astype(BF), preferred_element_type=F32
+    )
+    pair_at = pair_rank == (row % cap_src).astype(F32)
+    pair_select = jnp.where(pair_at, pair_member, 0.0).astype(BF)
+    pair_weighted = sum(
+        jnp.where(n & pair_at, facts_t[top_k + k : top_k + k + 1, :], 0.0)
+        for k, n in enumerate(pair_named)
+    )
+    slot_weight = jnp.sum(pair_weighted, axis=1, keepdims=True)
+
+    between = ("tp", "zy")
+    messages = token_messages(pair_select, tokens, mate_tokens, inv_rms, mate_inv, gain, chips)
+    arrived = exchange(messages, between).reshape(slots, half_dim)
+    grad_pair = jnp.concatenate([grad_out, mate_grad], axis=0)
     grad_rows = (
-        slot_weight * jnp.dot(select, grad_out, preferred_element_type=F32)
+        slot_weight * jnp.dot(pair_select, grad_pair, preferred_element_type=F32)
     ).astype(BF)
-    grad_blocks = exchange(blocks(grad_rows, experts))
+    grad_blocks = exchange(blocks(grad_rows, chips), between)
 
     own_pre = rounded(
         jnp.concatenate(
@@ -302,7 +347,7 @@
     parts = grad_parts(
         pre_send, other_pre, own_act, other_act, expert_out, gate_mat, up_mat, experts, top_k
     )
-    back = exchange(parts)
+    back = exchange(parts, ("tp", "zy", "core"))
 
     weight_high = rounded(weighted)
     weight_low = weighted - weight_high
@@ -321,19 +366,23 @@
 
 
 def solution(mesh):
+    sizes = mesh.shape
+    shape = (sizes["section"], sizes["tp"], sizes["ep"] // CORES, CORES)
+    fine = Mesh(mesh.devices.reshape(shape), ("section", "tp", "zy", "core"))
+    rows = ("tp", "zy", "core")
     return jax.shard_map(
         local,
-        mesh=mesh,
+        mesh=fine,
         in_specs=(
-            P(("tp", "ep"), "section"),
+            P(rows, "section"),
             P("section"),
-            P(("tp", "ep"), None),
-            P(("tp", "ep"), None),
-            P(("tp", "ep"), "section", None),
-            P(("tp", "ep"), "section", None),
-            P(("tp", "ep"), None, "section"),
-            P(("tp", "ep"), "section"),
+            P(rows, None),
+            P(rows, None),
+            P(rows, "section", None),
+            P(rows, "section", None),
+            P(rows, None, "section"),
+            P(rows, "section"),
         ),
-        out_specs=(P(("tp", "ep"), "section"), P(("tp", "ep"), "section"), P(("tp", "ep"), None)),
+        out_specs=(P(rows, "section"), P(rows, "section"), P(rows, None)),
         check_vma=False,
     )

time: 204 us -> 200 us (0.980)
  waiting for transfers between devices: 134 us -> 130 us
  local copies, waits for them, and re-layouts: 12 us -> 8.95 us
  other arithmetic: 1.98 us -> 4.7 us
    all_to_all x3, waiting for transfers between devices: 127 us -> 123 us  [exchange(): lax.all_to_all(blocked, axes, split_axis=0, concat_axis=0, tiled=True)]
  transfers between devices with their start and end apart: 6 -> 10, of which waited for: 4 -> 6; matrix products, arithmetic and copies ran while one was open for 7% -> 7% of each run, Pallas kernels for 1% -> 1%
where the time goes in v4:
time: 200 us
  waiting for transfers between devices  130 us (65%)
  starting transfers between devices  35.4 us (18%)
  Pallas kernels  11.6 us (6%)
  local copies, waits for them, and re-layouts  8.95 us (4%)
  matrix products  7.8 us (4%)
  other arithmetic  4.7 us (2%)
    all_to_all x3, waiting for transfers between devices, exchange(): lax.all_to_all(blocked, axes, split_axis=0, concat_axis=0, tiled=True)  123 us
    all_to_all x3, starting transfers between devices, exchange(): lax.all_to_all(blocked, axes, split_axis=0, concat_axis=0, tiled=True)  31.5 us
    ppermute x1, waiting for transfers between devices, local(): other_act = lax.ppermute(own_act, 'section', swap)  6.08 us
    unnamed x30, local copies, waits for them, and re-layouts  5.44 us
    pallas_call x1, Pallas kernels, grad_parts(): pl.pallas_call(body, grid=(half_dim // block,), in_specs=[whole(2 * ff_di...  4.27 us
  transfers between devices with their start and end apart: 10, of which 6 were waited for; matrix products, arithmetic and copies ran while one was open for 7% of the time, Pallas kernels for 1%

profile of v4, /device:TPU:2, one launch (start us, length us, event | category | flops | bytes accessed | tf_op | source)
XLA Modules:
  0.0 199.7 jit_solution(17808534058319687590)
XLA Ops:
  0.6 1.1 multiply_reduce_fusion.1
  1.7 1.7 collective-permute-start.2
  6.5 0.8 maximum_bitcast_fusion.1
  8.2 2.1 %token_messages.1 = bf16[64,4,2560]{2,1,0:T(4,128)(2,1)} custom-call(bf16[256,64]{1,0:T(8,128)(2,1)S(1)} %get-tuple-element.46.select_ref, bf16[32,2560]{1,0:T(8,128)(2,1)S(1)} %copy-done.5, bf16[32,2560]{1,0:T(8,128)(2,1)S(1)} %collective-permute-done.1.mate_ref, f32[32,1]{1,0:T(8,128)S(1)} %add_rsqrt_fusion.1.own_inv.refs_6_, ...), custom_call_target="tpu_custom_call" | custom-call | flops 1 | bytes 1 | tf_op jit(solution)/shard_map/token_messages/pallas_call | solution.py:48
  10.3 14.8 %all-to-all-start = ((bf16[64,4,2560]{2,1,0:T(4,128)(2,1)}), bf16[64,4,2560]{2,1,0:T(4,128)(2,1)S(1)}, u32[]{:S(2)}, u32[]{:S(2)}) async-start(bf16[64,4,2560]{2,1,0:T(4,128)(2,1)} %token_messages.1), calls=%async_computation | async-start | bytes 2621440 | tf_op jit(solution)/shard_map/all_to_all | solution.py:250
  25.6 1.0 collective-permute-done.5
  27.3 1.2 reshape.19
  28.5 32.4 %all-to-all-done = bf16[64,4,2560]{2,1,0:T(4,128)(2,1)S(1)} async-done(((bf16[64,4,2560]{2,1,0:T(4,128)(2,1)}), bf16[64,4,2560]{2,1,0:T(4,128)(2,1)S(1)}, u32[]{:S(2)}, u32[]{:S(2)}) %all-to-all-start) | async-done | bytes 1310752 | tf_op jit(solution)/shard_map/all_to_all | solution.py:250
  60.9 6.6 %all-to-all-start.1 = ((bf16[64,4,2560]{2,1,0:T(4,128)(2,1)}), bf16[64,4,2560]{2,1,0:T(4,128)(2,1)S(1)}, u32[]{:S(2)}, u32[]{:S(2)}) async-start(bf16[64,4,2560]{2,1,0:T(4,128)(2,1)} %reshape.19), calls=%async_computation.1 | async-start | bytes 2621440 | tf_op jit(solution)/shard_map/all_to_all | solution.py:250
  67.5 1.2 reshape.18
  68.8 3.8 %fusion.60 = f32[256,768]{1,0:T(8,128)S(1)} fusion(bf16[256,2560]{1,0:T(8,128)(2,1)} %reshape.18, bf16[1,2560,768]{2,1,0:T(8,128)(2,1)} %param.13), kind=kOutput, calls=%fused_computation.151 | convolution fusion | flops 1006632960 | bytes 6029312 | tf_op jit(solution)/shard_map/dot_general | solution.py:333
  72.8 1.2 fusion.62
  74.1 0.8 copy-done.8
  75.6 26.4 %all-to-all-done.1.rows_ref = bf16[64,4,2560]{2,1,0:T(4,128)(2,1)S(1)} async-done(((bf16[64,4,2560]{2,1,0:T(4,128)(2,1)}), bf16[64,4,2560]{2,1,0:T(4,128)(2,1)S(1)}, u32[]{:S(2)}, u32[]{:S(2)}) %all-to-all-start.1) | async-done | bytes 1310752 | tf_op jit(solution)/shard_map/all_to_all | solution.py:250
  101.9 2.1 %copy-done.1 = bf16[1,768,2560]{2,1,0:T(8,128)(2,1)S(1)} copy-done((bf16[1,768,2560]{2,1,0:T(8,128)(2,1)S(1)}, bf16[1,768,2560]{2,1,0:T(8,128)(2,1)}, u32[]{:S(2)}) %copy-start.1) | copy-done | bytes 3932184
  104.0 1.8 grad_act.1.refs_2_
  105.9 0.9 collective-permute-start.6
  107.3 1.2 convolution_convert_fusion.refs_4_
  108.5 6.1 %collective-permute-done.6.refs_3_ = bf16[256,768]{1,0:T(8,128)(2,1)S(1)} collective-permute-done((bf16[256,768]{1,0:T(8,128)(2,1)S(1)}, bf16[256,768]{1,0:T(8,128)(2,1)S(1)}, u32[]{:S(2)}, u32[]{:S(2)}) %collective-permute-start.6) | collective-permute-done | bytes 393248 | tf_op jit(solution)/shard_map/ppermute | solution.py:346
  114.6 4.3 %grad_parts.1 = bf16[128,2,5248]{2,1,0:T(2,128)(2,1)S(1)} custom-call(bf16[256,1536]{1,0:T(8,128)(2,1)S(1)} %fusion.1.refs_0_, bf16[256,1536]{1,0:T(8,128)(2,1)S(1)} %collective-permute-done.4.refs_1_, bf16[256,768]{1,0:T(8,128)(2,1)S(1)} %grad_act.1.refs_2_, bf16[256,768]{1,0:T(8,128)(2,1)S(1)} %collective-permute-done.6.refs_3_, ...), custom_call_target="tpu_custom_call" | custom-call | flops 1 | bytes 1 | tf_op jit(solution)/shard_map/grad_parts/pallas_call | solution.py:147
  118.9 1.5 copy-done
  120.4 10.1 %all-to-all-start.2 = ((bf16[128,2,5248]{2,1,0:T(2,128)(2,1)}), bf16[128,2,5248]{2,1,0:T(2,128)(2,1)S(1)}, u32[]{:S(2)}, u32[]{:S(2)}) async-start(bf16[128,2,5248]{2,1,0:T(2,128)(2,1)} %copy-done), calls=%async_computation.2 | async-start | bytes 5373952 | tf_op jit(solution)/shard_map/all_to_all | solution.py:250
  131.3 64.3 %all-to-all-done.2.refs_0_.refs_1_.refs_2_ = bf16[128,2,5248]{2,1,0:T(2,128)(2,1)S(1)} async-done(((bf16[128,2,5248]{2,1,0:T(2,128)(2,1)}), bf16[128,2,5248]{2,1,0:T(2,128)(2,1)S(1)}, u32[]{:S(2)}, u32[]{:S(2)}) %all-to-all-start.2) | async-done | bytes 2687008 | tf_op jit(solution)/shard_map/all_to_all | solution.py:250
  195.6 3.4 %finish.1 = (bf16[32,2560]{1,0:T(8,128)(2,1)}, bf16[32,2560]{1,0:T(8,128)(2,1)}, f32[32,128]{1,0:T(8,128)S(1)}) custom-call(bf16[128,2,5248]{2,1,0:T(2,128)(2,1)S(1)} %all-to-all-done.2.refs_0_.refs_1_.refs_2_, bf16[128,2,5248]{2,1,0:T(2,128)(2,1)S(1)} %all-to-all-done.2.refs_0_.refs_1_.refs_2_, ...), custom_call_target="tpu_custom_call" | custom-call | flops 1 | bytes 1 | tf_op jit(solution)/shard_map/finish/pallas_call | solution.py:214
  (72 shorter events, 8.1 us)
Async XLA Ops:
  1.7 4.4 %collective-permute-start.2 = (f32[32,1]{0,1:T(1,128)S(1)}, f32[32,1]{0,1:T(1,128)S(1)}, u32[]{:S(2)}, u32[]{:S(2)}) collective-permute-start(f32[32,1]{0,1:T(1,128)S(1)} %bitcast.81), channel_id=1, source_target_pairs={{0,128},{128,0},{1,129},{129,1},{2,130},{130,2},{3,131},{131,3},{4... | collective-permute-start | bytes 392 | tf_op jit(solution)/shard_map/ppermute | solution.py:288
  3.3 4.7 %collective-permute-start.3 = (f32[32,1]{0,1:T(1,128)S(1)}, f32[32,1]{0,1:T(1,128)S(1)}, u32[]{:S(2)}, u32[]{:S(2)}) collective-permute-start(f32[32,1]{0,1:T(1,128)S(1)} %bitcast.82), channel_id=1, source_target_pairs={{0,129},{1,128},{128,1},{129,0},{2,131},{3,130},{130,3},{131,2},{4... | collective-permute-start | bytes 392 | tf_op jit(solution)/shard_map/ppermute | solution.py:290
  3.3 4.6 %collective-permute-start.1 = (bf16[32,2560]{1,0:T(8,128)(2,1)}, bf16[32,2560]{1,0:T(8,128)(2,1)S(1)}, u32[]{:S(2)}, u32[]{:S(2)}) collective-permute-start(bf16[32,2560]{1,0:T(8,128)(2,1)} %refs_7_.1), channel_id=1, source_target_pairs={{0,1},{1,0},{2,3},{3,2},{4,5},{5,4},{6,7},{7,6},{8,9},{9,8},{10,11... | collective-permute-start | bytes 491528 | tf_op jit(solution)/shard_map/ppermute | solution.py:289
  5.3 1.2 collective-permute-start
  7.2 0.9 copy-start.5
  10.3 14.8 %copy-start.13 = (bf16[32,2560]{1,0:T(8,128)(2,1)S(1)}, bf16[32,2560]{1,0:T(8,128)(2,1)}, u32[]{:S(2)}) copy-start(bf16[32,2560]{1,0:T(8,128)(2,1)} %param.15) | copy-start | bytes 491524
  10.3 50.6 %all-to-all-start = ((bf16[64,4,2560]{2,1,0:T(4,128)(2,1)}), bf16[64,4,2560]{2,1,0:T(4,128)(2,1)S(1)}, u32[]{:S(2)}, u32[]{:S(2)}) async-start(bf16[64,4,2560]{2,1,0:T(4,128)(2,1)} %token_messages.1), calls=%async_computation | async-start | bytes 2621440 | tf_op jit(solution)/shard_map/all_to_all | solution.py:250
  25.1 1.5 collective-permute-start.5
  60.9 41.0 %all-to-all-start.1 = ((bf16[64,4,2560]{2,1,0:T(4,128)(2,1)}), bf16[64,4,2560]{2,1,0:T(4,128)(2,1)S(1)}, u32[]{:S(2)}, u32[]{:S(2)}) async-start(bf16[64,4,2560]{2,1,0:T(4,128)(2,1)} %reshape.19), calls=%async_computation.1 | async-start | bytes 2621440 | tf_op jit(solution)/shard_map/all_to_all | solution.py:250
  68.7 3.8 %copy-start.3 = (bf16[1,2560,768]{2,1,0:T(8,128)(2,1)S(1)}, bf16[1,2560,768]{2,1,0:T(8,128)(2,1)}, u32[]{:S(2)}) copy-start(bf16[1,2560,768]{2,1,0:T(8,128)(2,1)} %param.12) | copy-start | bytes 11796484
  68.8 4.1 %copy-start.10 = (bf16[256,2560]{1,0:T(8,128)(2,1)S(1)}, bf16[256,2560]{1,0:T(8,128)(2,1)}, u32[]{:S(2)}) copy-start(bf16[256,2560]{1,0:T(8,128)(2,1)} %reshape.18) | copy-start | bytes 3932164
  72.8 1.2 copy-start.6
  74.0 0.9 copy-start.8
  74.9 31.9 %collective-permute-start.4 = (bf16[256,1536]{1,0:T(8,128)(2,1)S(1)}, bf16[256,1536]{1,0:T(8,128)(2,1)S(1)}, u32[]{:S(2)}, u32[]{:S(2)}) collective-permute-start(bf16[256,1536]{1,0:T(8,128)(2,1)S(1)} %fusion.1.refs_0_), channel_id=1, source_target_pairs={{0,128},{128,0},{1,129},{129,1},{2,130},{130,2},{3,131},{131,3},{4... | collective-permute-start | bytes 2359304 | tf_op jit(solution)/shard_map/ppermute | solution.py:339
  101.9 2.1 %copy-start.1 = (bf16[1,768,2560]{2,1,0:T(8,128)(2,1)S(1)}, bf16[1,768,2560]{2,1,0:T(8,128)(2,1)}, u32[]{:S(2)}) copy-start(bf16[1,768,2560]{2,1,0:T(8,128)(2,1)} %param.14) | copy-start | bytes 11796484
  104.0 2.8 %copy-start.7 = (f32[256,768]{1,0:T(8,128)S(1)}, f32[256,768]{1,0:T(8,128)}, u32[]{:S(2)}) copy-start(f32[256,768]{1,0:T(8,128)} %copy-done.6) | copy-start | bytes 2359300
  104.0 2.8 %copy-start.9 = (f32[256,768]{1,0:T(8,128)S(1)}, f32[256,768]{1,0:T(8,128)}, u32[]{:S(2)}) copy-start(f32[256,768]{1,0:T(8,128)} %copy-done.8) | copy-start | bytes 2359300
  105.9 8.7 %collective-permute-start.6 = (bf16[256,768]{1,0:T(8,128)(2,1)S(1)}, bf16[256,768]{1,0:T(8,128)(2,1)S(1)}, u32[]{:S(2)}, u32[]{:S(2)}) collective-permute-start(bf16[256,768]{1,0:T(8,128)(2,1)S(1)} %grad_act.1.refs_2_), channel_id=1, source_target_pairs={{0,128},{128,0},{1,129},{129,1},{2,130},{130,2},{3,131},{131,3},{4... | collective-permute-start | bytes 1179656 | tf_op jit(solution)/shard_map/ppermute | solution.py:346
  107.0 7.5 %copy-start.4 = (bf16[1,2560,768]{2,1,0:T(8,128)(2,1)S(1)}, bf16[1,2560,768]{2,1,0:T(8,128)(2,1)}, u32[]{:S(2)}) copy-start(bf16[1,2560,768]{2,1,0:T(8,128)(2,1)} %param.12) | copy-start | bytes 11796484
  107.3 7.3 %copy-start.2 = (bf16[1,2560,768]{2,1,0:T(8,128)(2,1)S(1)}, bf16[1,2560,768]{2,1,0:T(8,128)(2,1)}, u32[]{:S(2)}) copy-start(bf16[1,2560,768]{2,1,0:T(8,128)(2,1)} %param.13) | copy-start | bytes 11796484
  118.9 1.5 copy-start
  120.4 10.1 %copy-start.11 = (f32[32,6]{0,1:T(8,128)S(1)}, f32[32,6]{0,1:T(8,128)}, u32[]{:S(2)}) copy-start(f32[32,6]{0,1:T(8,128)} %param.11) | copy-start | bytes 2308
  120.4 10.2 %copy-start.12 = (s32[32,6]{0,1:T(8,128)S(1)}, s32[32,6]{0,1:T(8,128)}, u32[]{:S(2)}) copy-start(s32[32,6]{0,1:T(8,128)} %param.10) | copy-start | bytes 2308
  120.4 75.2 %all-to-all-start.2 = ((bf16[128,2,5248]{2,1,0:T(2,128)(2,1)}), bf16[128,2,5248]{2,1,0:T(2,128)(2,1)S(1)}, u32[]{:S(2)}, u32[]{:S(2)}) async-start(bf16[128,2,5248]{2,1,0:T(2,128)(2,1)} %copy-done), calls=%async_computation.2 | async-start | bytes 5373952 | tf_op jit(solution)/shard_map/all_to_all | solution.py:250

commit v5 on v4

--- a/solution.py
+++ b/solution.py
@@ -262,6 +262,8 @@
     ff_dim = gate_mat.shape[1]
     swap = [(i, (i + 1) % section_size) for i in range(section_size)]
 
+    flip = [(0, 1), (1, 0)]
+    mate_routes = lax.ppermute(routes, "core", flip)
     routes_t = routes.T
     weights_t = route_weights.T
     slot = lax.broadcasted_iota(jnp.int32, (slots, tok_dev), 0)
@@ -279,7 +281,6 @@
         jnp.where(named[k] & at_rank, weights_t[k : k + 1, :], 0.0) for k in range(top_k)
     )
 
-    flip = [(0, 1), (1, 0)]
     core = lax.axis_index("core")
     chips = experts // CORES
     pair = CORES * tok_dev
@@ -288,20 +289,20 @@
     other_squares = lax.ppermute(squares, "section", swap)
     mate_tokens = lax.ppermute(tokens, "core", flip)
     mate_other = lax.ppermute(squares, ("section", "core"), [(i, 3 - i) for i in range(4)])
-    facts = jnp.concatenate([routes.astype(F32), route_weights], axis=1)
-    mate_facts = lax.ppermute(facts, "core", flip)
+    mate_weights = lax.ppermute(route_weights, "core", flip)
     mate_grad = lax.ppermute(grad_out, "core", flip)
     mate_f = mate_tokens.astype(F32)
     mate_squares = jnp.sum(mate_f * mate_f, axis=1, keepdims=True)
     inv_rms = lax.rsqrt((squares + other_squares) / full_dim + EPS)
     mate_inv = lax.rsqrt((mate_squares + mate_other) / full_dim + EPS)
 
-    facts_t = jnp.concatenate([facts, mate_facts], axis=0).T
+    pair_routes = jnp.concatenate([routes_t, mate_routes.T], axis=1)
+    pair_weights = jnp.concatenate([weights_t, mate_weights.T], axis=1)
     row = lax.broadcasted_iota(jnp.int32, (slots, pair), 0)
     column = lax.broadcasted_iota(jnp.int32, (slots, pair), 1)
-    wanted = (row // (CORES * cap_src) * CORES + core).astype(F32)
+    wanted = row // (CORES * cap_src) * CORES + core
     here = row // cap_src % CORES == (column // tok_dev + core) % CORES
-    pair_named = [(facts_t[k : k + 1, :] == wanted) & here for k in range(top_k)]
+    pair_named = [(pair_routes[k : k + 1, :] == wanted) & here for k in range(top_k)]
     pair_member = sum(n.astype(F32) for n in pair_named)
     before = lax.broadcasted_iota(jnp.int32, (pair, pair), 0)
     after = lax.broadcasted_iota(jnp.int32, (pair, pair), 1)
@@ -312,7 +313,7 @@
     pair_at = pair_rank == (row % cap_src).astype(F32)
     pair_select = jnp.where(pair_at, pair_member, 0.0).astype(BF)
     pair_weighted = sum(
-        jnp.where(n & pair_at, facts_t[top_k + k : top_k + k + 1, :], 0.0)
+        jnp.where(n & pair_at, pair_weights[k : k + 1, :], 0.0)
         for k, n in enumerate(pair_named)
     )
     slot_weight = jnp.sum(pair_weighted, axis=1, keepdims=True)

time: 200 us -> 199 us (level)
  transfers between devices with their start and end apart: 10 -> 11, of which waited for: 6 -> 6; matrix products, arithmetic and copies ran while one was open for 7% -> 7% of each run, Pallas kernels for 1% -> 1%
where the time goes in v5:
time: 199 us; the launch traced here: 198 us
  waiting for transfers between devices  130 us (65%)
  starting transfers between devices  36 us (18%)
  Pallas kernels  11.5 us (6%)
  local copies, waits for them, and re-layouts  8.97 us (5%)
  matrix products  7.79 us (4%)
  other arithmetic  3.37 us (2%)
    all_to_all x3, waiting for transfers between devices, exchange(): lax.all_to_all(blocked, axes, split_axis=0, concat_axis=0, tiled=True)  123 us
    all_to_all x3, starting transfers between devices, exchange(): lax.all_to_all(blocked, axes, split_axis=0, concat_axis=0, tiled=True)  31.5 us
    ppermute x1, waiting for transfers between devices, local(): other_act = lax.ppermute(own_act, 'section', swap)  6.09 us
    unnamed x30, local copies, waits for them, and re-layouts  5.44 us
    pallas_call x1, Pallas kernels, grad_parts(): pl.pallas_call(body, grid=(half_dim // block,), in_specs=[whole(2 * ff_di...  4.27 us
  transfers between devices with their start and end apart: 11, of which 6 were waited for; matrix products, arithmetic and copies ran while one was open for 7% of the time, Pallas kernels for 1%

profile of v5, /device:TPU:2, one launch (start us, length us, event | category | flops | bytes accessed | tf_op | source)
XLA Modules:
  0.0 198.4 jit_solution(866630614759130580)
XLA Ops:
  0.6 1.1 multiply_reduce_fusion.1
  1.7 1.7 collective-permute-start.2
  4.0 0.7 reshape.17.gain_ref.refs_8_
  5.4 0.8 pad_add_fusion
  7.1 2.0 %token_messages.1 = bf16[64,4,2560]{2,1,0:T(4,128)(2,1)} custom-call(bf16[256,64]{1,0:T(8,128)(2,1)S(1)} %get-tuple-element.46.select_ref, bf16[32,2560]{1,0:T(8,128)(2,1)S(1)} %copy-done.5, bf16[32,2560]{1,0:T(8,128)(2,1)S(1)} %collective-permute-done.1.mate_ref, f32[32,1]{1,0:T(8,128)S(1)} %add_rsqrt_fusion.1.own_inv.refs_6_, ...), custom_call_target="tpu_custom_call" | custom-call | flops 1 | bytes 1 | tf_op jit(solution)/shard_map/token_messages/pallas_call | solution.py:48
  9.2 14.8 %all-to-all-start = ((bf16[64,4,2560]{2,1,0:T(4,128)(2,1)}), bf16[64,4,2560]{2,1,0:T(4,128)(2,1)S(1)}, u32[]{:S(2)}, u32[]{:S(2)}) async-start(bf16[64,4,2560]{2,1,0:T(4,128)(2,1)} %token_messages.1), calls=%async_computation | async-start | bytes 2621440 | tf_op jit(solution)/shard_map/all_to_all | solution.py:250
  26.4 1.2 reshape.19
  27.7 31.9 %all-to-all-done = bf16[64,4,2560]{2,1,0:T(4,128)(2,1)S(1)} async-done(((bf16[64,4,2560]{2,1,0:T(4,128)(2,1)}), bf16[64,4,2560]{2,1,0:T(4,128)(2,1)S(1)}, u32[]{:S(2)}, u32[]{:S(2)}) %all-to-all-start) | async-done | bytes 1310752 | tf_op jit(solution)/shard_map/all_to_all | solution.py:250
  59.5 6.7 %all-to-all-start.1 = ((bf16[64,4,2560]{2,1,0:T(4,128)(2,1)}), bf16[64,4,2560]{2,1,0:T(4,128)(2,1)S(1)}, u32[]{:S(2)}, u32[]{:S(2)}) async-start(bf16[64,4,2560]{2,1,0:T(4,128)(2,1)} %reshape.19), calls=%async_computation.1 | async-start | bytes 2621440 | tf_op jit(solution)/shard_map/all_to_all | solution.py:250
  66.2 1.2 reshape.18
  67.5 3.8 %fusion.66 = f32[256,768]{1,0:T(8,128)S(1)} fusion(bf16[256,2560]{1,0:T(8,128)(2,1)} %reshape.18, bf16[1,2560,768]{2,1,0:T(8,128)(2,1)} %param.13), kind=kOutput, calls=%fused_computation.151 | convolution fusion | flops 1006632960 | bytes 6029312 | tf_op jit(solution)/shard_map/dot_general | solution.py:334
  71.5 1.2 fusion.68
  72.8 0.8 copy-done.8
  74.3 26.3 %all-to-all-done.1.rows_ref = bf16[64,4,2560]{2,1,0:T(4,128)(2,1)S(1)} async-done(((bf16[64,4,2560]{2,1,0:T(4,128)(2,1)}), bf16[64,4,2560]{2,1,0:T(4,128)(2,1)S(1)}, u32[]{:S(2)}, u32[]{:S(2)}) %all-to-all-start.1) | async-done | bytes 1310752 | tf_op jit(solution)/shard_map/all_to_all | solution.py:250
  100.6 2.1 %copy-done.1 = bf16[1,768,2560]{2,1,0:T(8,128)(2,1)S(1)} copy-done((bf16[1,768,2560]{2,1,0:T(8,128)(2,1)S(1)}, bf16[1,768,2560]{2,1,0:T(8,128)(2,1)}, u32[]{:S(2)}) %copy-start.1) | copy-done | bytes 3932184
  102.7 1.8 grad_act.1.refs_2_
  104.5 0.9 collective-permute-start.7
  106.0 1.2 convolution_convert_fusion.refs_4_
  107.2 6.1 %collective-permute-done.7.refs_3_ = bf16[256,768]{1,0:T(8,128)(2,1)S(1)} collective-permute-done((bf16[256,768]{1,0:T(8,128)(2,1)S(1)}, bf16[256,768]{1,0:T(8,128)(2,1)S(1)}, u32[]{:S(2)}, u32[]{:S(2)}) %collective-permute-start.7) | collective-permute-done | bytes 393248 | tf_op jit(solution)/shard_map/ppermute | solution.py:347
  113.3 4.3 %grad_parts.1 = bf16[128,2,5248]{2,1,0:T(2,128)(2,1)S(1)} custom-call(bf16[256,1536]{1,0:T(8,128)(2,1)S(1)} %fusion.1.refs_0_, bf16[256,1536]{1,0:T(8,128)(2,1)S(1)} %collective-permute-done.4.refs_1_, bf16[256,768]{1,0:T(8,128)(2,1)S(1)} %grad_act.1.refs_2_, bf16[256,768]{1,0:T(8,128)(2,1)S(1)} %collective-permute-done.7.refs_3_, ...), custom_call_target="tpu_custom_call" | custom-call | flops 1 | bytes 1 | tf_op jit(solution)/shard_map/grad_parts/pallas_call | solution.py:147
  117.5 1.5 copy-done
  119.1 10.1 %all-to-all-start.2 = ((bf16[128,2,5248]{2,1,0:T(2,128)(2,1)}), bf16[128,2,5248]{2,1,0:T(2,128)(2,1)S(1)}, u32[]{:S(2)}, u32[]{:S(2)}) async-start(bf16[128,2,5248]{2,1,0:T(2,128)(2,1)} %copy-done), calls=%async_computation.2 | async-start | bytes 5373952 | tf_op jit(solution)/shard_map/all_to_all | solution.py:250
  129.9 64.3 %all-to-all-done.2.refs_0_.refs_1_.refs_2_ = bf16[128,2,5248]{2,1,0:T(2,128)(2,1)S(1)} async-done(((bf16[128,2,5248]{2,1,0:T(2,128)(2,1)}), bf16[128,2,5248]{2,1,0:T(2,128)(2,1)S(1)}, u32[]{:S(2)}, u32[]{:S(2)}) %all-to-all-start.2) | async-done | bytes 2687008 | tf_op jit(solution)/shard_map/all_to_all | solution.py:250
  194.3 3.4 %finish.1 = (bf16[32,2560]{1,0:T(8,128)(2,1)}, bf16[32,2560]{1,0:T(8,128)(2,1)}, f32[32,128]{1,0:T(8,128)S(1)}) custom-call(bf16[128,2,5248]{2,1,0:T(2,128)(2,1)S(1)} %all-to-all-done.2.refs_0_.refs_1_.refs_2_, bf16[128,2,5248]{2,1,0:T(2,128)(2,1)S(1)} %all-to-all-done.2.refs_0_.refs_1_.refs_2_, ...), custom_call_target="tpu_custom_call" | custom-call | flops 1 | bytes 1 | tf_op jit(solution)/shard_map/finish/pallas_call | solution.py:214
  (73 shorter events, 7.6 us)
Async XLA Ops:
  1.7 3.6 %collective-permute-start.2 = (f32[32,1]{0,1:T(1,128)S(1)}, f32[32,1]{0,1:T(1,128)S(1)}, u32[]{:S(2)}, u32[]{:S(2)}) collective-permute-start(f32[32,1]{0,1:T(1,128)S(1)} %bitcast.85), channel_id=1, source_target_pairs={{0,128},{128,0},{1,129},{129,1},{2,130},{130,2},{3,131},{131,3},{4... | collective-permute-start | bytes 392 | tf_op jit(solution)/shard_map/ppermute | solution.py:289
  3.3 3.6 %collective-permute-start.3 = (f32[32,1]{0,1:T(1,128)S(1)}, f32[32,1]{0,1:T(1,128)S(1)}, u32[]{:S(2)}, u32[]{:S(2)}) collective-permute-start(f32[32,1]{0,1:T(1,128)S(1)} %bitcast.86), channel_id=1, source_target_pairs={{0,129},{1,128},{128,1},{129,0},{2,131},{3,130},{130,3},{131,2},{4... | collective-permute-start | bytes 392 | tf_op jit(solution)/shard_map/ppermute | solution.py:291
  3.3 3.5 %collective-permute-start.1 = (bf16[32,2560]{1,0:T(8,128)(2,1)}, bf16[32,2560]{1,0:T(8,128)(2,1)S(1)}, u32[]{:S(2)}, u32[]{:S(2)}) collective-permute-start(bf16[32,2560]{1,0:T(8,128)(2,1)} %refs_7_.1), channel_id=1, source_target_pairs={{0,1},{1,0},{2,3},{3,2},{4,5},{5,4},{6,7},{7,6},{8,9},{9,8},{10,11... | collective-permute-start | bytes 491528 | tf_op jit(solution)/shard_map/ppermute | solution.py:290
  3.9 1.5 collective-permute-start
  6.2 0.9 copy-start.5
  9.2 14.8 %copy-start.11 = (f32[32,6]{0,1:T(8,128)S(1)}, f32[32,6]{0,1:T(8,128)}, u32[]{:S(2)}) copy-start(f32[32,6]{0,1:T(8,128)} %param.11) | copy-start | bytes 2308
  9.2 14.9 %copy-start.13 = (bf16[32,2560]{1,0:T(8,128)(2,1)S(1)}, bf16[32,2560]{1,0:T(8,128)(2,1)}, u32[]{:S(2)}) copy-start(bf16[32,2560]{1,0:T(8,128)(2,1)} %param.15) | copy-start | bytes 491524
  9.2 50.4 %all-to-all-start = ((bf16[64,4,2560]{2,1,0:T(4,128)(2,1)}), bf16[64,4,2560]{2,1,0:T(4,128)(2,1)S(1)}, u32[]{:S(2)}, u32[]{:S(2)}) async-start(bf16[64,4,2560]{2,1,0:T(4,128)(2,1)} %token_messages.1), calls=%async_computation | async-start | bytes 2621440 | tf_op jit(solution)/shard_map/all_to_all | solution.py:250
  24.0 1.3 collective-permute-start.5
  24.1 1.6 collective-permute-start.6
  59.5 41.0 %all-to-all-start.1 = ((bf16[64,4,2560]{2,1,0:T(4,128)(2,1)}), bf16[64,4,2560]{2,1,0:T(4,128)(2,1)S(1)}, u32[]{:S(2)}, u32[]{:S(2)}) async-start(bf16[64,4,2560]{2,1,0:T(4,128)(2,1)} %reshape.19), calls=%async_computation.1 | async-start | bytes 2621440 | tf_op jit(solution)/shard_map/all_to_all | solution.py:250
  67.5 3.8 %copy-start.3 = (bf16[1,2560,768]{2,1,0:T(8,128)(2,1)S(1)}, bf16[1,2560,768]{2,1,0:T(8,128)(2,1)}, u32[]{:S(2)}) copy-start(bf16[1,2560,768]{2,1,0:T(8,128)(2,1)} %param.12) | copy-start | bytes 11796484
  67.5 4.1 %copy-start.10 = (bf16[256,2560]{1,0:T(8,128)(2,1)S(1)}, bf16[256,2560]{1,0:T(8,128)(2,1)}, u32[]{:S(2)}) copy-start(bf16[256,2560]{1,0:T(8,128)(2,1)} %reshape.18) | copy-start | bytes 3932164
  71.5 1.2 copy-start.6
  73.6 31.9 %collective-permute-start.4 = (bf16[256,1536]{1,0:T(8,128)(2,1)S(1)}, bf16[256,1536]{1,0:T(8,128)(2,1)S(1)}, u32[]{:S(2)}, u32[]{:S(2)}) collective-permute-start(bf16[256,1536]{1,0:T(8,128)(2,1)S(1)} %fusion.1.refs_0_), channel_id=1, source_target_pairs={{0,128},{128,0},{1,129},{129,1},{2,130},{130,2},{3,131},{131,3},{4... | collective-permute-start | bytes 2359304 | tf_op jit(solution)/shard_map/ppermute | solution.py:340
  100.6 2.1 %copy-start.1 = (bf16[1,768,2560]{2,1,0:T(8,128)(2,1)S(1)}, bf16[1,768,2560]{2,1,0:T(8,128)(2,1)}, u32[]{:S(2)}) copy-start(bf16[1,768,2560]{2,1,0:T(8,128)(2,1)} %param.14) | copy-start | bytes 11796484
  102.7 2.8 %copy-start.7 = (f32[256,768]{1,0:T(8,128)S(1)}, f32[256,768]{1,0:T(8,128)}, u32[]{:S(2)}) copy-start(f32[256,768]{1,0:T(8,128)} %copy-done.6) | copy-start | bytes 2359300
  102.7 2.8 %copy-start.9 = (f32[256,768]{1,0:T(8,128)S(1)}, f32[256,768]{1,0:T(8,128)}, u32[]{:S(2)}) copy-start(f32[256,768]{1,0:T(8,128)} %copy-done.8) | copy-start | bytes 2359300
  104.5 8.7 %collective-permute-start.7 = (bf16[256,768]{1,0:T(8,128)(2,1)S(1)}, bf16[256,768]{1,0:T(8,128)(2,1)S(1)}, u32[]{:S(2)}, u32[]{:S(2)}) collective-permute-start(bf16[256,768]{1,0:T(8,128)(2,1)S(1)} %grad_act.1.refs_2_), channel_id=1, source_target_pairs={{0,128},{128,0},{1,129},{129,1},{2,130},{130,2},{3,131},{131,3},{4... | collective-permute-start | bytes 1179656 | tf_op jit(solution)/shard_map/ppermute | solution.py:347
  105.7 7.5 %copy-start.4 = (bf16[1,2560,768]{2,1,0:T(8,128)(2,1)S(1)}, bf16[1,2560,768]{2,1,0:T(8,128)(2,1)}, u32[]{:S(2)}) copy-start(bf16[1,2560,768]{2,1,0:T(8,128)(2,1)} %param.12) | copy-start | bytes 11796484
  106.0 7.3 %copy-start.2 = (bf16[1,2560,768]{2,1,0:T(8,128)(2,1)S(1)}, bf16[1,2560,768]{2,1,0:T(8,128)(2,1)}, u32[]{:S(2)}) copy-start(bf16[1,2560,768]{2,1,0:T(8,128)(2,1)} %param.13) | copy-start | bytes 11796484
  117.5 1.5 copy-start
  119.1 10.2 %copy-start.12 = (s32[32,6]{0,1:T(8,128)S(1)}, s32[32,6]{0,1:T(8,128)}, u32[]{:S(2)}) copy-start(s32[32,6]{0,1:T(8,128)} %param.10) | copy-start | bytes 2308
  119.1 75.2 %all-to-all-start.2 = ((bf16[128,2,5248]{2,1,0:T(2,128)(2,1)}), bf16[128,2,5248]{2,1,0:T(2,128)(2,1)S(1)}, u32[]{:S(2)}, u32[]{:S(2)}) async-start(bf16[128,2,5248]{2,1,0:T(2,128)(2,1)} %copy-done), calls=%async_computation.2 | async-start | bytes 5373952 | tf_op jit(solution)/shard_map/all_to_all | solution.py:250
  (1 other events, 0.9 us)

commit v6 on v5

--- a/solution.py
+++ b/solution.py
@@ -27,7 +27,7 @@
 
 
 def column_block(width):
-    return 512 if width % 512 == 0 else width
+    return width // 2 if width % 256 == 0 else width
 
 
 def send_kernel(select_ref, own_ref, mate_ref, own_inv, mate_inv, gain_ref, out_ref):

time: 199 us -> 197 us (0.990)
  no operation moved by 1% of the time
where the time goes in v6:
time: 197 us
  waiting for transfers between devices  130 us (66%)
  starting transfers between devices  36 us (18%)
  Pallas kernels  9.93 us (5%)
  local copies, waits for them, and re-layouts  8.97 us (5%)
  matrix products  7.79 us (4%)
  other arithmetic  3.37 us (2%)
    all_to_all x3, waiting for transfers between devices, exchange(): lax.all_to_all(blocked, axes, split_axis=0, concat_axis=0, tiled=True)  123 us
    all_to_all x3, starting transfers between devices, exchange(): lax.all_to_all(blocked, axes, split_axis=0, concat_axis=0, tiled=True)  31.5 us
    ppermute x1, waiting for transfers between devices, local(): other_act = lax.ppermute(own_act, 'section', swap)  6.09 us
    unnamed x30, local copies, waits for them, and re-layouts  5.44 us
  transfers between devices with their start and end apart: 11, of which 6 were waited for; matrix products, arithmetic and copies ran while one was open for 7% of the time, Pallas kernels for 1%

profile of v6, /device:TPU:2, one launch (start us, length us, event | category | flops | bytes accessed | tf_op | source)
XLA Modules:
  0.0 196.8 jit_solution(9782986760494960170)
XLA Ops:
  0.6 1.1 multiply_reduce_fusion.1
  1.7 1.7 collective-permute-start.2
  4.0 0.7 reshape.17.gain_ref.refs_8_
  5.4 0.8 pad_add_fusion
  7.1 2.0 %token_messages.1 = bf16[64,4,2560]{2,1,0:T(4,128)(2,1)} custom-call(bf16[256,64]{1,0:T(8,128)(2,1)S(1)} %get-tuple-element.46.select_ref, bf16[32,2560]{1,0:T(8,128)(2,1)S(1)} %copy-done.5, bf16[32,2560]{1,0:T(8,128)(2,1)S(1)} %collective-permute-done.1.mate_ref, f32[32,1]{1,0:T(8,128)S(1)} %add_rsqrt_fusion.1.own_inv.refs_6_, ...), custom_call_target="tpu_custom_call" | custom-call | flops 1 | bytes 1 | tf_op jit(solution)/shard_map/token_messages/pallas_call | solution.py:48
  9.2 14.8 %all-to-all-start = ((bf16[64,4,2560]{2,1,0:T(4,128)(2,1)}), bf16[64,4,2560]{2,1,0:T(4,128)(2,1)S(1)}, u32[]{:S(2)}, u32[]{:S(2)}) async-start(bf16[64,4,2560]{2,1,0:T(4,128)(2,1)} %token_messages.1), calls=%async_computation | async-start | bytes 2621440 | tf_op jit(solution)/shard_map/all_to_all | solution.py:250
  26.4 1.2 reshape.19
  27.7 31.9 %all-to-all-done = bf16[64,4,2560]{2,1,0:T(4,128)(2,1)S(1)} async-done(((bf16[64,4,2560]{2,1,0:T(4,128)(2,1)}), bf16[64,4,2560]{2,1,0:T(4,128)(2,1)S(1)}, u32[]{:S(2)}, u32[]{:S(2)}) %all-to-all-start) | async-done | bytes 1310752 | tf_op jit(solution)/shard_map/all_to_all | solution.py:250
  59.5 6.7 %all-to-all-start.1 = ((bf16[64,4,2560]{2,1,0:T(4,128)(2,1)}), bf16[64,4,2560]{2,1,0:T(4,128)(2,1)S(1)}, u32[]{:S(2)}, u32[]{:S(2)}) async-start(bf16[64,4,2560]{2,1,0:T(4,128)(2,1)} %reshape.19), calls=%async_computation.1 | async-start | bytes 2621440 | tf_op jit(solution)/shard_map/all_to_all | solution.py:250
  66.2 1.2 reshape.18
  67.5 3.8 %fusion.66 = f32[256,768]{1,0:T(8,128)S(1)} fusion(bf16[256,2560]{1,0:T(8,128)(2,1)} %reshape.18, bf16[1,2560,768]{2,1,0:T(8,128)(2,1)} %param.13), kind=kOutput, calls=%fused_computation.151 | convolution fusion | flops 1006632960 | bytes 6029312 | tf_op jit(solution)/shard_map/dot_general | solution.py:334
  71.5 1.2 fusion.68
  72.8 0.8 copy-done.8
  74.3 26.3 %all-to-all-done.1.rows_ref = bf16[64,4,2560]{2,1,0:T(4,128)(2,1)S(1)} async-done(((bf16[64,4,2560]{2,1,0:T(4,128)(2,1)}), bf16[64,4,2560]{2,1,0:T(4,128)(2,1)S(1)}, u32[]{:S(2)}, u32[]{:S(2)}) %all-to-all-start.1) | async-done | bytes 1310752 | tf_op jit(solution)/shard_map/all_to_all | solution.py:250
  100.6 2.1 %copy-done.1 = bf16[1,768,2560]{2,1,0:T(8,128)(2,1)S(1)} copy-done((bf16[1,768,2560]{2,1,0:T(8,128)(2,1)S(1)}, bf16[1,768,2560]{2,1,0:T(8,128)(2,1)}, u32[]{:S(2)}) %copy-start.1) | copy-done | bytes 3932184
  102.7 1.8 grad_act.1.refs_2_
  104.5 0.9 collective-permute-start.7
  106.0 1.2 convolution_convert_fusion.refs_4_
  107.2 6.1 %collective-permute-done.7.refs_3_ = bf16[256,768]{1,0:T(8,128)(2,1)S(1)} collective-permute-done((bf16[256,768]{1,0:T(8,128)(2,1)S(1)}, bf16[256,768]{1,0:T(8,128)(2,1)S(1)}, u32[]{:S(2)}, u32[]{:S(2)}) %collective-permute-start.7) | collective-permute-done | bytes 393248 | tf_op jit(solution)/shard_map/ppermute | solution.py:347
  113.3 3.7 %grad_parts.1 = bf16[128,2,5248]{2,1,0:T(2,128)(2,1)S(1)} custom-call(bf16[256,1536]{1,0:T(8,128)(2,1)S(1)} %fusion.1.refs_0_, bf16[256,1536]{1,0:T(8,128)(2,1)S(1)} %collective-permute-done.4.refs_1_, bf16[256,768]{1,0:T(8,128)(2,1)S(1)} %grad_act.1.refs_2_, bf16[256,768]{1,0:T(8,128)(2,1)S(1)} %collective-permute-done.7.refs_3_, ...), custom_call_target="tpu_custom_call" | custom-call | flops 1 | bytes 1 | tf_op jit(solution)/shard_map/grad_parts/pallas_call | solution.py:147
  117.0 1.5 copy-done
  118.5 10.1 %all-to-all-start.2 = ((bf16[128,2,5248]{2,1,0:T(2,128)(2,1)}), bf16[128,2,5248]{2,1,0:T(2,128)(2,1)S(1)}, u32[]{:S(2)}, u32[]{:S(2)}) async-start(bf16[128,2,5248]{2,1,0:T(2,128)(2,1)} %copy-done), calls=%async_computation.2 | async-start | bytes 5373952 | tf_op jit(solution)/shard_map/all_to_all | solution.py:250
  129.3 64.3 %all-to-all-done.2.refs_0_.refs_1_.refs_2_ = bf16[128,2,5248]{2,1,0:T(2,128)(2,1)S(1)} async-done(((bf16[128,2,5248]{2,1,0:T(2,128)(2,1)}), bf16[128,2,5248]{2,1,0:T(2,128)(2,1)S(1)}, u32[]{:S(2)}, u32[]{:S(2)}) %all-to-all-start.2) | async-done | bytes 2687008 | tf_op jit(solution)/shard_map/all_to_all | solution.py:250
  193.7 2.4 %finish.1 = (bf16[32,2560]{1,0:T(8,128)(2,1)}, bf16[32,2560]{1,0:T(8,128)(2,1)}, f32[32,128]{1,0:T(8,128)S(1)}) custom-call(bf16[128,2,5248]{2,1,0:T(2,128)(2,1)S(1)} %all-to-all-done.2.refs_0_.refs_1_.refs_2_, bf16[128,2,5248]{2,1,0:T(2,128)(2,1)S(1)} %all-to-all-done.2.refs_0_.refs_1_.refs_2_, ...), custom_call_target="tpu_custom_call" | custom-call | flops 1 | bytes 1 | tf_op jit(solution)/shard_map/finish/pallas_call | solution.py:214
  (73 shorter events, 7.6 us)
Async XLA Ops:
  1.7 3.6 %collective-permute-start.2 = (f32[32,1]{0,1:T(1,128)S(1)}, f32[32,1]{0,1:T(1,128)S(1)}, u32[]{:S(2)}, u32[]{:S(2)}) collective-permute-start(f32[32,1]{0,1:T(1,128)S(1)} %bitcast.85), channel_id=1, source_target_pairs={{0,128},{128,0},{1,129},{129,1},{2,130},{130,2},{3,131},{131,3},{4... | collective-permute-start | bytes 392 | tf_op jit(solution)/shard_map/ppermute | solution.py:289
  3.3 3.6 %collective-permute-start.3 = (f32[32,1]{0,1:T(1,128)S(1)}, f32[32,1]{0,1:T(1,128)S(1)}, u32[]{:S(2)}, u32[]{:S(2)}) collective-permute-start(f32[32,1]{0,1:T(1,128)S(1)} %bitcast.86), channel_id=1, source_target_pairs={{0,129},{1,128},{128,1},{129,0},{2,131},{3,130},{130,3},{131,2},{4... | collective-permute-start | bytes 392 | tf_op jit(solution)/shard_map/ppermute | solution.py:291
  3.3 3.5 %collective-permute-start.1 = (bf16[32,2560]{1,0:T(8,128)(2,1)}, bf16[32,2560]{1,0:T(8,128)(2,1)S(1)}, u32[]{:S(2)}, u32[]{:S(2)}) collective-permute-start(bf16[32,2560]{1,0:T(8,128)(2,1)} %refs_7_.1), channel_id=1, source_target_pairs={{0,1},{1,0},{2,3},{3,2},{4,5},{5,4},{6,7},{7,6},{8,9},{9,8},{10,11... | collective-permute-start | bytes 491528 | tf_op jit(solution)/shard_map/ppermute | solution.py:290
  3.9 1.5 collective-permute-start
  6.2 0.9 copy-start.5
  9.2 14.8 %copy-start.11 = (f32[32,6]{0,1:T(8,128)S(1)}, f32[32,6]{0,1:T(8,128)}, u32[]{:S(2)}) copy-start(f32[32,6]{0,1:T(8,128)} %param.11) | copy-start | bytes 2308
  9.2 14.9 %copy-start.13 = (bf16[32,2560]{1,0:T(8,128)(2,1)S(1)}, bf16[32,2560]{1,0:T(8,128)(2,1)}, u32[]{:S(2)}) copy-start(bf16[32,2560]{1,0:T(8,128)(2,1)} %param.15) | copy-start | bytes 491524
  9.2 50.4 %all-to-all-start = ((bf16[64,4,2560]{2,1,0:T(4,128)(2,1)}), bf16[64,4,2560]{2,1,0:T(4,128)(2,1)S(1)}, u32[]{:S(2)}, u32[]{:S(2)}) async-start(bf16[64,4,2560]{2,1,0:T(4,128)(2,1)} %token_messages.1), calls=%async_computation | async-start | bytes 2621440 | tf_op jit(solution)/shard_map/all_to_all | solution.py:250
  24.0 1.3 collective-permute-start.5
  24.1 1.6 collective-permute-start.6
  59.5 41.0 %all-to-all-start.1 = ((bf16[64,4,2560]{2,1,0:T(4,128)(2,1)}), bf16[64,4,2560]{2,1,0:T(4,128)(2,1)S(1)}, u32[]{:S(2)}, u32[]{:S(2)}) async-start(bf16[64,4,2560]{2,1,0:T(4,128)(2,1)} %reshape.19), calls=%async_computation.1 | async-start | bytes 2621440 | tf_op jit(solution)/shard_map/all_to_all | solution.py:250
  67.5 3.8 %copy-start.3 = (bf16[1,2560,768]{2,1,0:T(8,128)(2,1)S(1)}, bf16[1,2560,768]{2,1,0:T(8,128)(2,1)}, u32[]{:S(2)}) copy-start(bf16[1,2560,768]{2,1,0:T(8,128)(2,1)} %param.12) | copy-start | bytes 11796484
  67.5 4.1 %copy-start.10 = (bf16[256,2560]{1,0:T(8,128)(2,1)S(1)}, bf16[256,2560]{1,0:T(8,128)(2,1)}, u32[]{:S(2)}) copy-start(bf16[256,2560]{1,0:T(8,128)(2,1)} %reshape.18) | copy-start | bytes 3932164
  71.5 1.2 copy-start.6
  73.6 31.9 %collective-permute-start.4 = (bf16[256,1536]{1,0:T(8,128)(2,1)S(1)}, bf16[256,1536]{1,0:T(8,128)(2,1)S(1)}, u32[]{:S(2)}, u32[]{:S(2)}) collective-permute-start(bf16[256,1536]{1,0:T(8,128)(2,1)S(1)} %fusion.1.refs_0_), channel_id=1, source_target_pairs={{0,128},{128,0},{1,129},{129,1},{2,130},{130,2},{3,131},{131,3},{4... | collective-permute-start | bytes 2359304 | tf_op jit(solution)/shard_map/ppermute | solution.py:340
  100.6 2.1 %copy-start.1 = (bf16[1,768,2560]{2,1,0:T(8,128)(2,1)S(1)}, bf16[1,768,2560]{2,1,0:T(8,128)(2,1)}, u32[]{:S(2)}) copy-start(bf16[1,768,2560]{2,1,0:T(8,128)(2,1)} %param.14) | copy-start | bytes 11796484
  102.7 2.8 %copy-start.7 = (f32[256,768]{1,0:T(8,128)S(1)}, f32[256,768]{1,0:T(8,128)}, u32[]{:S(2)}) copy-start(f32[256,768]{1,0:T(8,128)} %copy-done.6) | copy-start | bytes 2359300
  102.7 2.8 %copy-start.9 = (f32[256,768]{1,0:T(8,128)S(1)}, f32[256,768]{1,0:T(8,128)}, u32[]{:S(2)}) copy-start(f32[256,768]{1,0:T(8,128)} %copy-done.8) | copy-start | bytes 2359300
  104.5 8.7 %collective-permute-start.7 = (bf16[256,768]{1,0:T(8,128)(2,1)S(1)}, bf16[256,768]{1,0:T(8,128)(2,1)S(1)}, u32[]{:S(2)}, u32[]{:S(2)}) collective-permute-start(bf16[256,768]{1,0:T(8,128)(2,1)S(1)} %grad_act.1.refs_2_), channel_id=1, source_target_pairs={{0,128},{128,0},{1,129},{129,1},{2,130},{130,2},{3,131},{131,3},{4... | collective-permute-start | bytes 1179656 | tf_op jit(solution)/shard_map/ppermute | solution.py:347
  105.7 7.5 %copy-start.4 = (bf16[1,2560,768]{2,1,0:T(8,128)(2,1)S(1)}, bf16[1,2560,768]{2,1,0:T(8,128)(2,1)}, u32[]{:S(2)}) copy-start(bf16[1,2560,768]{2,1,0:T(8,128)(2,1)} %param.12) | copy-start | bytes 11796484
  106.0 7.3 %copy-start.2 = (bf16[1,2560,768]{2,1,0:T(8,128)(2,1)S(1)}, bf16[1,2560,768]{2,1,0:T(8,128)(2,1)}, u32[]{:S(2)}) copy-start(bf16[1,2560,768]{2,1,0:T(8,128)(2,1)} %param.13) | copy-start | bytes 11796484
  117.0 1.5 copy-start
  118.5 10.2 %copy-start.12 = (s32[32,6]{0,1:T(8,128)S(1)}, s32[32,6]{0,1:T(8,128)}, u32[]{:S(2)}) copy-start(s32[32,6]{0,1:T(8,128)} %param.10) | copy-start | bytes 2308
  118.5 75.2 %all-to-all-start.2 = ((bf16[128,2,5248]{2,1,0:T(2,128)(2,1)}), bf16[128,2,5248]{2,1,0:T(2,128)(2,1)S(1)}, u32[]{:S(2)}, u32[]{:S(2)}) async-start(bf16[128,2,5248]{2,1,0:T(2,128)(2,1)} %copy-done), calls=%async_computation.2 | async-start | bytes 5373952 | tf_op jit(solution)/shard_map/all_to_all | solution.py:250
  (1 other events, 0.9 us)

commit v7 on v6

--- a/solution.py
+++ b/solution.py
@@ -76,10 +76,10 @@
     peers, per_peer, half_dim = rows.shape
     slots = peers * per_peer
     ff_dim = down_mat.shape[0]
-    block = ff_dim // 3
+    block = ff_dim // 2
     return pl.pallas_call(
         act_kernel,
-        grid=(3,),
+        grid=(2,),
         in_specs=[
             pl.BlockSpec((peers, per_peer, half_dim), lambda i: (0, 0, 0)),
             pl.BlockSpec((block, half_dim), lambda i: (i, 0)),

time: 197 us -> 198 us (level)
  no operation moved by 1% of the time
where the time goes in v7:
time: 198 us; the launch traced here: 197 us
  waiting for transfers between devices  130 us (66%)
  starting transfers between devices  36 us (18%)
  Pallas kernels  10.1 us (5%)
  local copies, waits for them, and re-layouts  8.97 us (5%)
  matrix products  7.79 us (4%)
  other arithmetic  3.37 us (2%)
    all_to_all x3, waiting for transfers between devices, exchange(): lax.all_to_all(blocked, axes, split_axis=0, concat_axis=0, tiled=True)  123 us
    all_to_all x3, starting transfers between devices, exchange(): lax.all_to_all(blocked, axes, split_axis=0, concat_axis=0, tiled=True)  31.5 us
    ppermute x1, waiting for transfers between devices, local(): other_act = lax.ppermute(own_act, 'section', swap)  6.09 us
    unnamed x30, local copies, waits for them, and re-layouts  5.44 us
  transfers between devices with their start and end apart: 11, of which 6 were waited for; matrix products, arithmetic and copies ran while one was open for 7% of the time, Pallas kernels for 1%

profile of v7, /device:TPU:2, one launch (start us, length us, event | category | flops | bytes accessed | tf_op | source)
XLA Modules:
  0.0 196.9 jit_solution(5871832977153227035)
XLA Ops:
  0.6 1.1 multiply_reduce_fusion.1
  1.7 1.7 collective-permute-start.2
  4.0 0.7 reshape.17.gain_ref.refs_8_
  5.4 0.8 pad_add_fusion
  7.1 2.0 %token_messages.1 = bf16[64,4,2560]{2,1,0:T(4,128)(2,1)} custom-call(bf16[256,64]{1,0:T(8,128)(2,1)S(1)} %get-tuple-element.46.select_ref, bf16[32,2560]{1,0:T(8,128)(2,1)S(1)} %copy-done.5, bf16[32,2560]{1,0:T(8,128)(2,1)S(1)} %collective-permute-done.1.mate_ref, f32[32,1]{1,0:T(8,128)S(1)} %add_rsqrt_fusion.1.own_inv.refs_6_, ...), custom_call_target="tpu_custom_call" | custom-call | flops 1 | bytes 1 | tf_op jit(solution)/shard_map/token_messages/pallas_call | solution.py:48
  9.2 14.8 %all-to-all-start = ((bf16[64,4,2560]{2,1,0:T(4,128)(2,1)}), bf16[64,4,2560]{2,1,0:T(4,128)(2,1)S(1)}, u32[]{:S(2)}, u32[]{:S(2)}) async-start(bf16[64,4,2560]{2,1,0:T(4,128)(2,1)} %token_messages.1), calls=%async_computation | async-start | bytes 2621440 | tf_op jit(solution)/shard_map/all_to_all | solution.py:250
  26.4 1.2 reshape.19
  27.7 31.9 %all-to-all-done = bf16[64,4,2560]{2,1,0:T(4,128)(2,1)S(1)} async-done(((bf16[64,4,2560]{2,1,0:T(4,128)(2,1)}), bf16[64,4,2560]{2,1,0:T(4,128)(2,1)S(1)}, u32[]{:S(2)}, u32[]{:S(2)}) %all-to-all-start) | async-done | bytes 1310752 | tf_op jit(solution)/shard_map/all_to_all | solution.py:250
  59.5 6.7 %all-to-all-start.1 = ((bf16[64,4,2560]{2,1,0:T(4,128)(2,1)}), bf16[64,4,2560]{2,1,0:T(4,128)(2,1)S(1)}, u32[]{:S(2)}, u32[]{:S(2)}) async-start(bf16[64,4,2560]{2,1,0:T(4,128)(2,1)} %reshape.19), calls=%async_computation.1 | async-start | bytes 2621440 | tf_op jit(solution)/shard_map/all_to_all | solution.py:250
  66.2 1.2 reshape.18
  67.5 3.8 %fusion.66 = f32[256,768]{1,0:T(8,128)S(1)} fusion(bf16[256,2560]{1,0:T(8,128)(2,1)} %reshape.18, bf16[1,2560,768]{2,1,0:T(8,128)(2,1)} %param.13), kind=kOutput, calls=%fused_computation.151 | convolution fusion | flops 1006632960 | bytes 6029312 | tf_op jit(solution)/shard_map/dot_general | solution.py:334
  71.5 1.2 fusion.68
  72.8 0.8 copy-done.8
  74.3 26.3 %all-to-all-done.1.rows_ref = bf16[64,4,2560]{2,1,0:T(4,128)(2,1)S(1)} async-done(((bf16[64,4,2560]{2,1,0:T(4,128)(2,1)}), bf16[64,4,2560]{2,1,0:T(4,128)(2,1)S(1)}, u32[]{:S(2)}, u32[]{:S(2)}) %all-to-all-start.1) | async-done | bytes 1310752 | tf_op jit(solution)/shard_map/all_to_all | solution.py:250
  100.6 2.1 %copy-done.1 = bf16[1,768,2560]{2,1,0:T(8,128)(2,1)S(1)} copy-done((bf16[1,768,2560]{2,1,0:T(8,128)(2,1)S(1)}, bf16[1,768,2560]{2,1,0:T(8,128)(2,1)}, u32[]{:S(2)}) %copy-start.1) | copy-done | bytes 3932184
  102.7 1.9 grad_act.1.refs_2_
  104.6 0.9 collective-permute-start.7
  106.1 1.2 convolution_convert_fusion.refs_4_
  107.3 6.1 %collective-permute-done.7.refs_3_ = bf16[256,768]{1,0:T(8,128)(2,1)S(1)} collective-permute-done((bf16[256,768]{1,0:T(8,128)(2,1)S(1)}, bf16[256,768]{1,0:T(8,128)(2,1)S(1)}, u32[]{:S(2)}, u32[]{:S(2)}) %collective-permute-start.7) | collective-permute-done | bytes 393248 | tf_op jit(solution)/shard_map/ppermute | solution.py:347
  113.4 3.7 %grad_parts.1 = bf16[128,2,5248]{2,1,0:T(2,128)(2,1)S(1)} custom-call(bf16[256,1536]{1,0:T(8,128)(2,1)S(1)} %fusion.1.refs_0_, bf16[256,1536]{1,0:T(8,128)(2,1)S(1)} %collective-permute-done.4.refs_1_, bf16[256,768]{1,0:T(8,128)(2,1)S(1)} %grad_act.1.refs_2_, bf16[256,768]{1,0:T(8,128)(2,1)S(1)} %collective-permute-done.7.refs_3_, ...), custom_call_target="tpu_custom_call" | custom-call | flops 1 | bytes 1 | tf_op jit(solution)/shard_map/grad_parts/pallas_call | solution.py:147
  117.1 1.5 copy-done
  118.6 10.1 %all-to-all-start.2 = ((bf16[128,2,5248]{2,1,0:T(2,128)(2,1)}), bf16[128,2,5248]{2,1,0:T(2,128)(2,1)S(1)}, u32[]{:S(2)}, u32[]{:S(2)}) async-start(bf16[128,2,5248]{2,1,0:T(2,128)(2,1)} %copy-done), calls=%async_computation.2 | async-start | bytes 5373952 | tf_op jit(solution)/shard_map/all_to_all | solution.py:250
  129.5 64.3 %all-to-all-done.2.refs_0_.refs_1_.refs_2_ = bf16[128,2,5248]{2,1,0:T(2,128)(2,1)S(1)} async-done(((bf16[128,2,5248]{2,1,0:T(2,128)(2,1)}), bf16[128,2,5248]{2,1,0:T(2,128)(2,1)S(1)}, u32[]{:S(2)}, u32[]{:S(2)}) %all-to-all-start.2) | async-done | bytes 2687008 | tf_op jit(solution)/shard_map/all_to_all | solution.py:250
  193.8 2.4 %finish.1 = (bf16[32,2560]{1,0:T(8,128)(2,1)}, bf16[32,2560]{1,0:T(8,128)(2,1)}, f32[32,128]{1,0:T(8,128)S(1)}) custom-call(bf16[128,2,5248]{2,1,0:T(2,128)(2,1)S(1)} %all-to-all-done.2.refs_0_.refs_1_.refs_2_, bf16[128,2,5248]{2,1,0:T(2,128)(2,1)S(1)} %all-to-all-done.2.refs_0_.refs_1_.refs_2_, ...), custom_call_target="tpu_custom_call" | custom-call | flops 1 | bytes 1 | tf_op jit(solution)/shard_map/finish/pallas_call | solution.py:214
  (73 shorter events, 7.6 us)
Async XLA Ops:
  1.7 3.6 %collective-permute-start.2 = (f32[32,1]{0,1:T(1,128)S(1)}, f32[32,1]{0,1:T(1,128)S(1)}, u32[]{:S(2)}, u32[]{:S(2)}) collective-permute-start(f32[32,1]{0,1:T(1,128)S(1)} %bitcast.85), channel_id=1, source_target_pairs={{0,128},{128,0},{1,129},{129,1},{2,130},{130,2},{3,131},{131,3},{4... | collective-permute-start | bytes 392 | tf_op jit(solution)/shard_map/ppermute | solution.py:289
  3.3 3.6 %collective-permute-start.3 = (f32[32,1]{0,1:T(1,128)S(1)}, f32[32,1]{0,1:T(1,128)S(1)}, u32[]{:S(2)}, u32[]{:S(2)}) collective-permute-start(f32[32,1]{0,1:T(1,128)S(1)} %bitcast.86), channel_id=1, source_target_pairs={{0,129},{1,128},{128,1},{129,0},{2,131},{3,130},{130,3},{131,2},{4... | collective-permute-start | bytes 392 | tf_op jit(solution)/shard_map/ppermute | solution.py:291
  3.3 3.5 %collective-permute-start.1 = (bf16[32,2560]{1,0:T(8,128)(2,1)}, bf16[32,2560]{1,0:T(8,128)(2,1)S(1)}, u32[]{:S(2)}, u32[]{:S(2)}) collective-permute-start(bf16[32,2560]{1,0:T(8,128)(2,1)} %refs_7_.1), channel_id=1, source_target_pairs={{0,1},{1,0},{2,3},{3,2},{4,5},{5,4},{6,7},{7,6},{8,9},{9,8},{10,11... | collective-permute-start | bytes 491528 | tf_op jit(solution)/shard_map/ppermute | solution.py:290
  3.9 1.5 collective-permute-start
  6.2 0.9 copy-start.5
  9.2 14.8 %copy-start.11 = (f32[32,6]{0,1:T(8,128)S(1)}, f32[32,6]{0,1:T(8,128)}, u32[]{:S(2)}) copy-start(f32[32,6]{0,1:T(8,128)} %param.11) | copy-start | bytes 2308
  9.2 14.9 %copy-start.13 = (bf16[32,2560]{1,0:T(8,128)(2,1)S(1)}, bf16[32,2560]{1,0:T(8,128)(2,1)}, u32[]{:S(2)}) copy-start(bf16[32,2560]{1,0:T(8,128)(2,1)} %param.15) | copy-start | bytes 491524
  9.2 50.4 %all-to-all-start = ((bf16[64,4,2560]{2,1,0:T(4,128)(2,1)}), bf16[64,4,2560]{2,1,0:T(4,128)(2,1)S(1)}, u32[]{:S(2)}, u32[]{:S(2)}) async-start(bf16[64,4,2560]{2,1,0:T(4,128)(2,1)} %token_messages.1), calls=%async_computation | async-start | bytes 2621440 | tf_op jit(solution)/shard_map/all_to_all | solution.py:250
  24.0 1.3 collective-permute-start.5
  24.1 1.6 collective-permute-start.6
  59.5 41.0 %all-to-all-start.1 = ((bf16[64,4,2560]{2,1,0:T(4,128)(2,1)}), bf16[64,4,2560]{2,1,0:T(4,128)(2,1)S(1)}, u32[]{:S(2)}, u32[]{:S(2)}) async-start(bf16[64,4,2560]{2,1,0:T(4,128)(2,1)} %reshape.19), calls=%async_computation.1 | async-start | bytes 2621440 | tf_op jit(solution)/shard_map/all_to_all | solution.py:250
  67.5 3.8 %copy-start.3 = (bf16[1,2560,768]{2,1,0:T(8,128)(2,1)S(1)}, bf16[1,2560,768]{2,1,0:T(8,128)(2,1)}, u32[]{:S(2)}) copy-start(bf16[1,2560,768]{2,1,0:T(8,128)(2,1)} %param.12) | copy-start | bytes 11796484
  67.5 4.1 %copy-start.10 = (bf16[256,2560]{1,0:T(8,128)(2,1)S(1)}, bf16[256,2560]{1,0:T(8,128)(2,1)}, u32[]{:S(2)}) copy-start(bf16[256,2560]{1,0:T(8,128)(2,1)} %reshape.18) | copy-start | bytes 3932164
  71.5 1.2 copy-start.6
  73.6 32.0 %collective-permute-start.4 = (bf16[256,1536]{1,0:T(8,128)(2,1)S(1)}, bf16[256,1536]{1,0:T(8,128)(2,1)S(1)}, u32[]{:S(2)}, u32[]{:S(2)}) collective-permute-start(bf16[256,1536]{1,0:T(8,128)(2,1)S(1)} %fusion.1.refs_0_), channel_id=1, source_target_pairs={{0,128},{128,0},{1,129},{129,1},{2,130},{130,2},{3,131},{131,3},{4... | collective-permute-start | bytes 2359304 | tf_op jit(solution)/shard_map/ppermute | solution.py:340
  100.6 2.1 %copy-start.1 = (bf16[1,768,2560]{2,1,0:T(8,128)(2,1)S(1)}, bf16[1,768,2560]{2,1,0:T(8,128)(2,1)}, u32[]{:S(2)}) copy-start(bf16[1,768,2560]{2,1,0:T(8,128)(2,1)} %param.14) | copy-start | bytes 11796484
  102.7 2.9 %copy-start.7 = (f32[256,768]{1,0:T(8,128)S(1)}, f32[256,768]{1,0:T(8,128)}, u32[]{:S(2)}) copy-start(f32[256,768]{1,0:T(8,128)} %copy-done.6) | copy-start | bytes 2359300
  102.7 2.9 %copy-start.9 = (f32[256,768]{1,0:T(8,128)S(1)}, f32[256,768]{1,0:T(8,128)}, u32[]{:S(2)}) copy-start(f32[256,768]{1,0:T(8,128)} %copy-done.8) | copy-start | bytes 2359300
  104.6 8.7 %collective-permute-start.7 = (bf16[256,768]{1,0:T(8,128)(2,1)S(1)}, bf16[256,768]{1,0:T(8,128)(2,1)S(1)}, u32[]{:S(2)}, u32[]{:S(2)}) collective-permute-start(bf16[256,768]{1,0:T(8,128)(2,1)S(1)} %grad_act.1.refs_2_), channel_id=1, source_target_pairs={{0,128},{128,0},{1,129},{129,1},{2,130},{130,2},{3,131},{131,3},{4... | collective-permute-start | bytes 1179656 | tf_op jit(solution)/shard_map/ppermute | solution.py:347
  105.8 7.5 %copy-start.4 = (bf16[1,2560,768]{2,1,0:T(8,128)(2,1)S(1)}, bf16[1,2560,768]{2,1,0:T(8,128)(2,1)}, u32[]{:S(2)}) copy-start(bf16[1,2560,768]{2,1,0:T(8,128)(2,1)} %param.12) | copy-start | bytes 11796484
  106.1 7.3 %copy-start.2 = (bf16[1,2560,768]{2,1,0:T(8,128)(2,1)S(1)}, bf16[1,2560,768]{2,1,0:T(8,128)(2,1)}, u32[]{:S(2)}) copy-start(bf16[1,2560,768]{2,1,0:T(8,128)(2,1)} %param.13) | copy-start | bytes 11796484
  117.1 1.5 copy-start
  118.6 10.2 %copy-start.12 = (s32[32,6]{0,1:T(8,128)S(1)}, s32[32,6]{0,1:T(8,128)}, u32[]{:S(2)}) copy-start(s32[32,6]{0,1:T(8,128)} %param.10) | copy-start | bytes 2308
  118.6 75.2 %all-to-all-start.2 = ((bf16[128,2,5248]{2,1,0:T(2,128)(2,1)}), bf16[128,2,5248]{2,1,0:T(2,128)(2,1)S(1)}, u32[]{:S(2)}, u32[]{:S(2)}) async-start(bf16[128,2,5248]{2,1,0:T(2,128)(2,1)} %copy-done), calls=%async_computation.2 | async-start | bytes 5373952 | tf_op jit(solution)/shard_map/all_to_all | solution.py:250
  (1 other events, 0.9 us)
